TPU v7x, 1024 devices: a whole 4x8x16 slice. The times are simulated.
1024 devices in a mesh: dp: 256 (over x, z_hi, y, core), group: 4 (over z_lo).
Axes of the slice: x: 4, y: 8, z: 16 (z_hi: 4, z_lo: 4; z = z_hi * 4 + z_lo), core: 2. Of those that a mesh axis runs over, the one named last changes fastest.
Arguments:
- image_emb: bfloat16 [262144, 1152], P(('dp', 'group')), may hold values from -0.1796875 to 0.1796875
- text_emb: bfloat16 [262144, 1152], P(('dp', 'group')), may hold values from -0.1796875 to 0.1796875
- scale: float32 [1], replicated, may hold values from 4 to 12
- bias: float32 [1], replicated, may hold values from -4 to -1
Outputs:
- row_loss: float32 [262144], P(('dp', 'group'))
- grad_image: float32 [262144, 1152], P(('dp', 'group'))
- grad_text: float32 [262144, 1152], P(('dp', 'group'))
All inputs are finite; a program needn't handle non-finite values.
Results may differ from a plain program's by a relative error of at most 0.0039.
Values may be sent and summed in bfloat16 or wider, within the bound.
No kernel may reach another device: no remote copies, remote signals or barrier semaphores. Data moves between devices by JAX's collectives and lax.ppermute only.
A program may use at most 32 MiB of HBM per device.

v0:
```python
import jax
import jax.numpy as jnp
from jax import lax
from jax.sharding import PartitionSpec as P

HOPS = 4


def shifted(value, axis, steps):
    count = lax.axis_size(axis)
    pairs = [(source, (source + steps) % count) for source in range(count)]
    return lax.ppermute(value, axis, pairs)


def unit_rows(emb):
    values = emb.astype(jnp.float32)
    norm = jnp.sqrt(jnp.sum(values * values, axis=-1, keepdims=True) + 1e-06)
    return (values / norm, norm)


def back_norm(grad, unit, norm):
    return (grad - unit * jnp.sum(unit * grad, axis=-1, keepdims=True)) / norm


def tile_terms(images, texts, step, s_val, b_val):
    logits = (
        s_val
        * lax.dot_general(
            images, texts, (((1,), (1,)), ((), ())), preferred_element_type=jnp.float32
        )
        + b_val
    )
    rows = images.shape[0]
    if step == 0:
        upper = lax.broadcasted_iota(jnp.int32, (rows, rows), 0)
        lower = lax.broadcasted_iota(jnp.int32, (rows, rows), 1)
        sign = jnp.where(upper == lower, 1.0, -1.0).astype(jnp.float32)
    else:
        sign = -jnp.ones((rows, rows), jnp.float32)
    partial_loss = jnp.sum(jax.nn.softplus(-sign * logits), axis=-1)
    coef = (-sign * jax.nn.sigmoid(-sign * logits)).astype(jnp.bfloat16)
    return (coef, partial_loss)


def column_sum(coef, images):
    return lax.dot_general(
        coef, images, (((0,), (0,)), ((), ())), preferred_element_type=jnp.float32
    )


def shards(image_emb, text_emb, scale, bias):
    image_unit, image_norm = unit_rows(image_emb)
    text_unit, text_norm = unit_rows(text_emb)
    images = image_unit.astype(jnp.bfloat16)
    own_texts = text_unit.astype(jnp.bfloat16)
    s_val = scale[0]
    b_val = bias[0]
    rows = images.shape[0]
    width = images.shape[1]
    grad_x = jnp.zeros((rows, width), jnp.float32)
    losses = jnp.zeros((rows,), jnp.float32)
    texts = own_texts
    carried = jnp.zeros((rows, width), jnp.float32)
    for step in range(HOPS):
        if step > 0:
            texts = shifted(texts, ("dp", "group"), 1)
            carried = shifted(carried, ("dp", "group"), 1)
        coef, partial_loss = tile_terms(images, texts, step, s_val, b_val)
        losses = losses + partial_loss
        grad_x = grad_x + s_val * jnp.dot(coef, texts, preferred_element_type=jnp.float32)
        carried = carried + s_val * column_sum(coef, images)
    grad_y = shifted(carried, ("dp", "group"), 1 - HOPS)
    row_loss = losses / (HOPS * rows)
    grad_image = back_norm(grad_x, image_unit, image_norm)
    grad_text = back_norm(grad_y, text_unit, text_norm)
    return (row_loss, grad_image, grad_text)


def solution(mesh):
    in_specs = (P(("dp", "group"), None), P(("dp", "group"), None), P(), P())
    out_specs = (P(("dp", "group")), P(("dp", "group"), None), P(("dp", "group"), None))
    return jax.shard_map(shards, mesh=mesh, in_specs=in_specs, out_specs=out_specs, check_vma=False)
```

profile of v0, /device:TPU:64, one launch (start us, length us, event | category | flops | bytes accessed | tf_op | source)
XLA Modules:
  0.0 202.5 jit_solution(15862375550125152975)
XLA Ops:
  1.3 1.3 fusion.2
  2.6 1.3 fusion.13
  5.0 0.5 fusion.9
  5.9 4.3 %collective-permute-start.3 = (f32[256,1152]{1,0:T(8,128)S(1)}, f32[256,1152]{1,0:T(8,128)S(1)}, u32[]{:S(2)}, u32[]{:S(2)}) collective-permute-start(f32[256,1152]{1,0:T(8,128)S(1)} %convolution_multiply_fusion.3), channel_id=1, source_target_pairs={{0,1},{1,2},{2,3},{3,4},{4,5},{5,6},{6,7},{7,8},{8,9},{9,10},{10,1... | collective-permute-start | bytes 3538952 | tf_op jit(solution)/shard_map/ppermute | solution.py:12
  10.2 4.3 %collective-permute-start = (bf16[256,1152]{1,0:T(8,128)(2,1)S(1)}, bf16[256,1152]{1,0:T(8,128)(2,1)S(1)}, u32[]{:S(2)}, u32[]{:S(2)}) collective-permute-start(bf16[256,1152]{1,0:T(8,128)(2,1)S(1)} %fusion.14), channel_id=1, source_target_pairs={{0,1},{1,2},{2,3},{3,4},{4,5},{5,6},{6,7},{7,8},{8,9},{9,10},{10,1... | collective-permute-start | bytes 1769480 | tf_op jit(solution)/shard_map/ppermute | solution.py:12
  14.5 33.7 %collective-permute-done = bf16[256,1152]{1,0:T(8,128)(2,1)S(1)} collective-permute-done((bf16[256,1152]{1,0:T(8,128)(2,1)S(1)}, bf16[256,1152]{1,0:T(8,128)(2,1)S(1)}, u32[]{:S(2)}, u32[]{:S(2)}) %collective-permute-start) | collective-permute-done | bytes 589856 | tf_op jit(solution)/shard_map/ppermute | solution.py:12
  48.2 0.5 fusion.10
  49.0 4.3 %collective-permute-start.4 = (f32[256,1152]{1,0:T(8,128)S(1)}, f32[256,1152]{1,0:T(8,128)S(1)}, u32[]{:S(2)}, u32[]{:S(2)}) collective-permute-start(f32[256,1152]{1,0:T(8,128)S(1)} %fusion.1), channel_id=1, source_target_pairs={{0,1},{1,2},{2,3},{3,4},{4,5},{5,6},{6,7},{7,8},{8,9},{9,10},{10,1... | collective-permute-start | bytes 3538952 | tf_op jit(solution)/shard_map/ppermute | solution.py:12
  53.3 4.3 %collective-permute-start.1 = (bf16[256,1152]{1,0:T(8,128)(2,1)S(1)}, bf16[256,1152]{1,0:T(8,128)(2,1)S(1)}, u32[]{:S(2)}, u32[]{:S(2)}) collective-permute-start(bf16[256,1152]{1,0:T(8,128)(2,1)S(1)} %collective-permute-done), channel_id=1, source_target_pairs={{0,1},{1,2},{2,3},{3,4},{4,5},{5,6},{6,7},{7,8},{8,9},{9,10},{10,1... | collective-permute-start | bytes 1769480 | tf_op jit(solution)/shard_map/ppermute | solution.py:12
  57.6 33.8 %collective-permute-done.1 = bf16[256,1152]{1,0:T(8,128)(2,1)S(1)} collective-permute-done((bf16[256,1152]{1,0:T(8,128)(2,1)S(1)}, bf16[256,1152]{1,0:T(8,128)(2,1)S(1)}, u32[]{:S(2)}, u32[]{:S(2)}) %collective-permute-start.1) | collective-permute-done | bytes 589856 | tf_op jit(solution)/shard_map/ppermute | solution.py:12
  91.4 0.5 fusion.11
  92.4 3.3 %collective-permute-start.5 = (f32[256,1152]{1,0:T(8,128)S(1)}, f32[256,1152]{1,0:T(8,128)S(1)}, u32[]{:S(2)}, u32[]{:S(2)}) collective-permute-start(f32[256,1152]{1,0:T(8,128)S(1)} %add.108), channel_id=1, source_target_pairs={{0,1},{1,2},{2,3},{3,4},{4,5},{5,6},{6,7},{7,8},{8,9},{9,10},{10,1... | collective-permute-start | bytes 3538952 | tf_op jit(solution)/shard_map/ppermute | solution.py:12
  95.7 0.4 fusion.15
  96.1 5.3 %collective-permute-start.2 = (bf16[256,1152]{1,0:T(8,128)(2,1)S(1)}, bf16[256,1152]{1,0:T(8,128)(2,1)S(1)}, u32[]{:S(2)}, u32[]{:S(2)}) collective-permute-start(bf16[256,1152]{1,0:T(8,128)(2,1)S(1)} %collective-permute-done.1), channel_id=1, source_target_pairs={{0,1},{1,2},{2,3},{3,4},{4,5},{5,6},{6,7},{7,8},{8,9},{9,10},{10,1... | collective-permute-start | bytes 1769480 | tf_op jit(solution)/shard_map/ppermute | solution.py:12
  101.4 0.4 convolution_add_fusion.2
  101.8 0.4 convolution_add_fusion.1
  102.2 31.2 %collective-permute-done.2 = bf16[256,1152]{1,0:T(8,128)(2,1)S(1)} collective-permute-done((bf16[256,1152]{1,0:T(8,128)(2,1)S(1)}, bf16[256,1152]{1,0:T(8,128)(2,1)S(1)}, u32[]{:S(2)}, u32[]{:S(2)}) %collective-permute-start.2) | collective-permute-done | bytes 589856 | tf_op jit(solution)/shard_map/ppermute | solution.py:12
  133.5 0.5 fusion.12
  134.5 17.6 %collective-permute-start.6 = (f32[256,1152]{1,0:T(8,128)S(1)}, f32[256,1152]{1,0:T(8,128)S(1)}, u32[]{:S(2)}, u32[]{:S(2)}) collective-permute-start(f32[256,1152]{1,0:T(8,128)S(1)} %add.109), channel_id=1, source_target_pairs={{0,1021},{1,1022},{2,1023},{3,0},{4,1},{5,2},{6,3},{7,4},{8,5},{9,... | collective-permute-start | bytes 3538952 | tf_op jit(solution)/shard_map/ppermute | solution.py:12
  152.1 0.6 add_multiply_fusion
  152.7 0.5 multiply_reduce_fusion.1
  153.3 1.3 subtract_divide_fusion.1
  154.6 46.3 %collective-permute-done.6 = f32[256,1152]{1,0:T(8,128)S(1)} collective-permute-done((f32[256,1152]{1,0:T(8,128)S(1)}, f32[256,1152]{1,0:T(8,128)S(1)}, u32[]{:S(2)}, u32[]{:S(2)}) %collective-permute-start.6) | collective-permute-done | bytes 1179680 | tf_op jit(solution)/shard_map/ppermute | solution.py:12
  201.2 1.3 subtract_divide_fusion
  (18 shorter events, 2.5 us)
Async XLA Ops:
  0.6 3.3 %copy-start = (bf16[256,1152]{1,0:T(8,128)(2,1)S(1)}, bf16[256,1152]{1,0:T(8,128)(2,1)}, u32[]{:S(2)}) copy-start(bf16[256,1152]{1,0:T(8,128)(2,1)} %param.5) | copy-start | bytes 1769476
  5.9 42.8 %collective-permute-start.3 = (f32[256,1152]{1,0:T(8,128)S(1)}, f32[256,1152]{1,0:T(8,128)S(1)}, u32[]{:S(2)}, u32[]{:S(2)}) collective-permute-start(f32[256,1152]{1,0:T(8,128)S(1)} %convolution_multiply_fusion.3), channel_id=1, source_target_pairs={{0,1},{1,2},{2,3},{3,4},{4,5},{5,6},{6,7},{7,8},{8,9},{9,10},{10,1... | collective-permute-start | bytes 3538952 | tf_op jit(solution)/shard_map/ppermute | solution.py:12
  10.2 38.0 %collective-permute-start = (bf16[256,1152]{1,0:T(8,128)(2,1)S(1)}, bf16[256,1152]{1,0:T(8,128)(2,1)S(1)}, u32[]{:S(2)}, u32[]{:S(2)}) collective-permute-start(bf16[256,1152]{1,0:T(8,128)(2,1)S(1)} %fusion.14), channel_id=1, source_target_pairs={{0,1},{1,2},{2,3},{3,4},{4,5},{5,6},{6,7},{7,8},{8,9},{9,10},{10,1... | collective-permute-start | bytes 1769480 | tf_op jit(solution)/shard_map/ppermute | solution.py:12
  49.0 43.2 %collective-permute-start.4 = (f32[256,1152]{1,0:T(8,128)S(1)}, f32[256,1152]{1,0:T(8,128)S(1)}, u32[]{:S(2)}, u32[]{:S(2)}) collective-permute-start(f32[256,1152]{1,0:T(8,128)S(1)} %fusion.1), channel_id=1, source_target_pairs={{0,1},{1,2},{2,3},{3,4},{4,5},{5,6},{6,7},{7,8},{8,9},{9,10},{10,1... | collective-permute-start | bytes 3538952 | tf_op jit(solution)/shard_map/ppermute | solution.py:12
  53.3 38.1 %collective-permute-start.1 = (bf16[256,1152]{1,0:T(8,128)(2,1)S(1)}, bf16[256,1152]{1,0:T(8,128)(2,1)S(1)}, u32[]{:S(2)}, u32[]{:S(2)}) collective-permute-start(bf16[256,1152]{1,0:T(8,128)(2,1)S(1)} %collective-permute-done), channel_id=1, source_target_pairs={{0,1},{1,2},{2,3},{3,4},{4,5},{5,6},{6,7},{7,8},{8,9},{9,10},{10,1... | collective-permute-start | bytes 1769480 | tf_op jit(solution)/shard_map/ppermute | solution.py:12
  92.4 41.9 %collective-permute-start.5 = (f32[256,1152]{1,0:T(8,128)S(1)}, f32[256,1152]{1,0:T(8,128)S(1)}, u32[]{:S(2)}, u32[]{:S(2)}) collective-permute-start(f32[256,1152]{1,0:T(8,128)S(1)} %add.108), channel_id=1, source_target_pairs={{0,1},{1,2},{2,3},{3,4},{4,5},{5,6},{6,7},{7,8},{8,9},{9,10},{10,1... | collective-permute-start | bytes 3538952 | tf_op jit(solution)/shard_map/ppermute | solution.py:12
  96.1 37.3 %collective-permute-start.2 = (bf16[256,1152]{1,0:T(8,128)(2,1)S(1)}, bf16[256,1152]{1,0:T(8,128)(2,1)S(1)}, u32[]{:S(2)}, u32[]{:S(2)}) collective-permute-start(bf16[256,1152]{1,0:T(8,128)(2,1)S(1)} %collective-permute-done.1), channel_id=1, source_target_pairs={{0,1},{1,2},{2,3},{3,4},{4,5},{5,6},{6,7},{7,8},{8,9},{9,10},{10,1... | collective-permute-start | bytes 1769480 | tf_op jit(solution)/shard_map/ppermute | solution.py:12
  134.3 18.4 %copy-start.1 = (bf16[256,1152]{1,0:T(8,128)(2,1)S(1)}, bf16[256,1152]{1,0:T(8,128)(2,1)}, u32[]{:S(2)}) copy-start(bf16[256,1152]{1,0:T(8,128)(2,1)} %param.4) | copy-start | bytes 1769476
  134.5 66.4 %collective-permute-start.6 = (f32[256,1152]{1,0:T(8,128)S(1)}, f32[256,1152]{1,0:T(8,128)S(1)}, u32[]{:S(2)}, u32[]{:S(2)}) collective-permute-start(f32[256,1152]{1,0:T(8,128)S(1)} %add.109), channel_id=1, source_target_pairs={{0,1021},{1,1022},{2,1023},{3,0},{4,1},{5,2},{6,3},{7,4},{8,5},{9,... | collective-permute-start | bytes 3538952 | tf_op jit(solution)/shard_map/ppermute | solution.py:12
where the time goes:
time: 203 us
  waiting for transfers between devices  145 us (71%)
  starting transfers between devices  43.3 us (21%)
  other arithmetic  6.71 us (3%)
  matrix products  5.27 us (3%)
  between operations  2.17 us (1%)
    ppermute x7, waiting for transfers between devices, shifted(): return lax.ppermute(value, axis, pairs)  145 us
    ppermute x7, starting transfers between devices, shifted(): return lax.ppermute(value, axis, pairs)  43.3 us
  transfers between devices with their start and end apart: 7, of which 4 were waited for; matrix products, arithmetic and copies ran while one was open for 3% of the time, Pallas kernels for 0%

commit v1 on v0

v1 whole, which is shorter than its diff:
```python
import jax
import jax.numpy as jnp
from jax import lax
from jax.sharding import PartitionSpec as P

HOPS = 4
GROUP = 4
AXES = ("dp", "group")


def routes(lines):
    def at(line, place):
        return (line % lines) * GROUP + place

    text, near, far = [], [], []
    for line in range(lines):
        text += [
            (at(line, 0), at(line, 1)),
            (at(line, 1), at(line + 1, 0)),
            (at(line, 3), at(line, 2)),
            (at(line, 2), at(line, 3)),
        ]
        near += [
            (at(line, 2), at(line, 1)),
            (at(line + 1, 1), at(line, 2)),
        ]
        far += [
            (at(line, 3), at(line, 1)),
            (at(line + 1, 0), at(line, 2)),
            (at(line, 1), at(line, 0)),
            (at(line + 1, 2), at(line, 3)),
        ]
    return (text, near, far)


def back(pairs):
    return [(target, source) for source, target in pairs]


def unit_rows(emb):
    values = emb.astype(jnp.float32)
    norm = jnp.sqrt(jnp.sum(values * values, axis=-1, keepdims=True) + 1e-06)
    return (values / norm, norm)


def unit_bf(emb):
    return unit_rows(emb)[0].astype(jnp.bfloat16)


def back_norm(grad, unit, norm):
    return (grad - unit * jnp.sum(unit * grad, axis=-1, keepdims=True)) / norm


def rows_by_rows(a, b):
    return lax.dot_general(a, b, (((1,), (1,)), ((), ())), preferred_element_type=jnp.float32)


def columns_by_rows(a, b):
    return lax.dot_general(a, b, (((0,), (0,)), ((), ())), preferred_element_type=jnp.float32)


def off_terms(images, texts, s_val, b_val, keep):
    logits = s_val * rows_by_rows(images, texts) + b_val
    loss = jnp.sum(jax.nn.softplus(logits), axis=-1)
    coef = jax.nn.sigmoid(logits).astype(jnp.bfloat16)
    return (jnp.where(keep, coef, 0), jnp.where(keep, loss, 0.0))


def own_terms(images, texts, s_val, b_val):
    logits = s_val * rows_by_rows(images, texts) + b_val
    rows = images.shape[0]
    upper = lax.broadcasted_iota(jnp.int32, (rows, rows), 0)
    lower = lax.broadcasted_iota(jnp.int32, (rows, rows), 1)
    sign = jnp.where(upper == lower, 1.0, -1.0).astype(jnp.float32)
    loss = jnp.sum(jax.nn.softplus(-sign * logits), axis=-1)
    coef = (-sign * jax.nn.sigmoid(-sign * logits)).astype(jnp.bfloat16)
    return (coef, loss)


def shards(image_emb, text_emb, scale, bias):
    text_way, near_way, far_way = routes(lax.axis_size("dp"))
    place = lax.axis_index("group")
    hub = (place == 1) | (place == 2)
    s_val = scale[0]
    b_val = bias[0]
    rows = image_emb.shape[0]

    near_raw = lax.ppermute(image_emb, AXES, near_way)
    text_raw = lax.ppermute(text_emb, AXES, text_way)
    far_raw = lax.ppermute(image_emb, AXES, far_way)

    image_unit, image_norm = unit_rows(image_emb)
    text_unit, text_norm = unit_rows(text_emb)
    images = image_unit.astype(jnp.bfloat16)
    texts = text_unit.astype(jnp.bfloat16)
    coef, loss = own_terms(images, texts, s_val, b_val)
    grad_x = jnp.dot(coef, texts, preferred_element_type=jnp.float32)
    grad_y = columns_by_rows(coef, images)

    other = unit_bf(text_raw)
    near = jnp.where(hub, unit_bf(near_raw), images)
    far = unit_bf(far_raw)

    c_on, l_on = off_terms(near, texts, s_val, b_val, hub)
    c_rn, l_rn = off_terms(near, other, s_val, b_val, True)
    grad_near = s_val * (
        jnp.dot(c_on, texts, preferred_element_type=jnp.float32)
        + jnp.dot(c_rn, other, preferred_element_type=jnp.float32)
    )
    loss_near = l_on + l_rn
    near_back = lax.ppermute(grad_near.astype(jnp.bfloat16), AXES, back(near_way))

    c_of, l_of = off_terms(far, texts, s_val, b_val, True)
    c_rf, l_rf = off_terms(far, other, s_val, b_val, hub)
    grad_far = s_val * (
        jnp.dot(c_of, texts, preferred_element_type=jnp.float32)
        + jnp.dot(c_rf, other, preferred_element_type=jnp.float32)
    )
    far_back = lax.ppermute(grad_far.astype(jnp.bfloat16), AXES, back(far_way))
    grad_other = s_val * (columns_by_rows(c_rn, near) + columns_by_rows(c_rf, far))
    text_back = lax.ppermute(grad_other.astype(jnp.bfloat16), AXES, back(text_way))
    loss_near_back = lax.ppermute(loss_near, AXES, back(near_way))
    loss_far_back = lax.ppermute(l_of + l_rf, AXES, back(far_way))

    grad_y = s_val * (grad_y + columns_by_rows(c_on, near) + columns_by_rows(c_of, far))
    grad_y = grad_y + text_back.astype(jnp.float32)
    grad_x = s_val * grad_x + jnp.where(hub, near_back.astype(jnp.float32), grad_near)
    grad_x = grad_x + far_back.astype(jnp.float32)
    loss = loss + jnp.where(hub, loss_near_back, loss_near) + loss_far_back
    row_loss = loss / (HOPS * rows)
    grad_image = back_norm(grad_x, image_unit, image_norm)
    grad_text = back_norm(grad_y, text_unit, text_norm)
    return (row_loss, grad_image, grad_text)


def solution(mesh):
    in_specs = (P(("dp", "group"), None), P(("dp", "group"), None), P(), P())
    out_specs = (P(("dp", "group")), P(("dp", "group"), None), P(("dp", "group"), None))
    return jax.shard_map(shards, mesh=mesh, in_specs=in_specs, out_specs=out_specs, check_vma=False)
```

time: 203 us -> 97 us (0.48)
  the two profiles are of different devices: /device:TPU:64 before, /device:TPU:128 now
where the time goes in v1:
time: 97 us; the launch traced here: 96.6 us
  starting transfers between devices  44.4 us (46%)
  waiting for transfers between devices  35.6 us (37%)
  matrix products  7.3 us (8%)
  other arithmetic  7.13 us (7%)
  between operations  2.16 us (2%)
    ppermute x1, starting transfers between devices, shards(): far_raw = lax.ppermute(image_emb, AXES, far_way)  21.1 us
    ppermute x1, waiting for transfers between devices, shards(): text_raw = lax.ppermute(text_emb, AXES, text_way)  12.7 us
    ppermute x1, waiting for transfers between devices, shards(): far_back = lax.ppermute(grad_far.astype(jnp.bfloat16), AXES, back(far_way))  12 us
    ppermute x1, waiting for transfers between devices, shards(): loss_near_back = lax.ppermute(loss_near, AXES, back(near_way))  10.9 us
    ppermute x1, starting transfers between devices, shards(): lax.ppermute(grad_near.astype(jnp.bfloat16), AXES, back(near_way))  10.6 us
    reduce_sum x5, other arithmetic, unit_rows(): norm = jnp.sqrt(jnp.sum(values * values, axis=-1, keepdims=True) + 1e-06)  3.11 us
    ppermute x1, starting transfers between devices, shards(): far_back = lax.ppermute(grad_far.astype(jnp.bfloat16), AXES, back(far_way))  3.09 us
    dot_general x5, matrix products, rows_by_rows(): lax.dot_general(a, b, (((1,), (1,)), ((), ())), preferred_element_type=jn...  2.89 us
  transfers between devices with their start and end apart: 8, of which 3 were waited for; matrix products, arithmetic and copies ran while one was open for 11% of the time, Pallas kernels for 0%

profile of v1, /device:TPU:128, one launch (start us, length us, event | category | flops | bytes accessed | tf_op | source)
XLA Modules:
  0.0 96.6 jit_solution(12179038045658799729)
XLA Ops:
  0.7 21.1 %collective-permute-start.3 = (bf16[256,1152]{1,0:T(8,128)(2,1)}, bf16[256,1152]{1,0:T(8,128)(2,1)S(1)}, u32[]{:S(2)}, u32[]{:S(2)}) collective-permute-start(bf16[256,1152]{1,0:T(8,128)(2,1)} %param.4), channel_id=1, source_target_pairs={{3,1},{4,2},{1,0},{6,3},{7,5},{8,6},{5,4},{10,7},{11,9},{12,10},{9... | collective-permute-start | bytes 1769480 | tf_op jit(solution)/shard_map/ppermute | solution.py:90
  21.7 1.9 %collective-permute-start = (bf16[256,1152]{1,0:T(8,128)(2,1)}, bf16[256,1152]{1,0:T(8,128)(2,1)S(1)}, u32[]{:S(2)}, u32[]{:S(2)}) collective-permute-start(bf16[256,1152]{1,0:T(8,128)(2,1)} %param.4), channel_id=1, source_target_pairs={{2,1},{5,2},{6,5},{9,6},{10,9},{13,10},{14,13},{17,14},{18,17},{21... | collective-permute-start | bytes 1769480 | tf_op jit(solution)/shard_map/ppermute | solution.py:88
  23.7 1.9 %collective-permute-start.1 = (bf16[256,1152]{1,0:T(8,128)(2,1)}, bf16[256,1152]{1,0:T(8,128)(2,1)S(1)}, u32[]{:S(2)}, u32[]{:S(2)}) collective-permute-start(bf16[256,1152]{1,0:T(8,128)(2,1)} %param.5), channel_id=1, source_target_pairs={{0,1},{1,4},{3,2},{2,3},{4,5},{5,8},{7,6},{6,7},{8,9},{9,12},{11,1... | collective-permute-start | bytes 1769480 | tf_op jit(solution)/shard_map/ppermute | solution.py:89
  25.6 1.3 %fusion.7 = f32[256]{0:T(256)S(1)} fusion(bf16[256,1152]{1,0:T(8,128)(2,1)} %param.4), kind=kLoop, calls=%fused_computation.23 | loop fusion | flops 884480 | bytes 590848 | tf_op jit(solution)/shard_map/reduce_sum | solution.py:42
  26.9 1.3 %fusion.8 = f32[256]{0:T(256)S(1)} fusion(bf16[256,1152]{1,0:T(8,128)(2,1)} %param.5), kind=kLoop, calls=%fused_computation.24 | loop fusion | flops 884480 | bytes 590848 | tf_op jit(solution)/shard_map/reduce_sum | solution.py:42
  29.5 0.6 fusion.22
  30.1 0.5 fusion.29
  31.2 12.7 %collective-permute-done.1 = bf16[256,1152]{1,0:T(8,128)(2,1)S(1)} collective-permute-done((bf16[256,1152]{1,0:T(8,128)(2,1)}, bf16[256,1152]{1,0:T(8,128)(2,1)S(1)}, u32[]{:S(2)}, u32[]{:S(2)}) %collective-permute-start.1) | collective-permute-done | bytes 589856 | tf_op jit(solution)/shard_map/ppermute | solution.py:89
  44.4 0.6 fusion.26
  45.8 0.5 fusion.24
  46.7 1.9 %collective-permute-start.7 = (bf16[256,1152]{1,0:T(8,128)(2,1)S(1)}, bf16[256,1152]{1,0:T(8,128)(2,1)S(1)}, u32[]{:S(2)}, u32[]{:S(2)}) collective-permute-start(bf16[256,1152]{1,0:T(8,128)(2,1)S(1)} %fusion.5), channel_id=1, source_target_pairs={{1,0},{4,1},{2,3},{3,2},{5,4},{8,5},{6,7},{7,6},{9,8},{12,9},{10,1... | collective-permute-start | bytes 1769480 | tf_op jit(solution)/shard_map/ppermute | solution.py:121
  48.6 0.5 fusion.23
  50.4 10.6 %collective-permute-start.5 = (bf16[256,1152]{1,0:T(8,128)(2,1)S(1)}, bf16[256,1152]{1,0:T(8,128)(2,1)S(1)}, u32[]{:S(2)}, u32[]{:S(2)}) collective-permute-start(bf16[256,1152]{1,0:T(8,128)(2,1)S(1)} %get-tuple-element.15), channel_id=1, source_target_pairs={{1,2},{2,5},{5,6},{6,9},{9,10},{10,13},{13,14},{14,17},{17,18},{18... | collective-permute-start | bytes 1769480 | tf_op jit(solution)/shard_map/ppermute | solution.py:111
  61.0 0.6 fusion.25
  62.1 1.9 %collective-permute-start.2 = (f32[256]{0:T(256)S(1)}, f32[256]{0:T(256)S(1)}, u32[]{:S(2)}, u32[]{:S(2)}) collective-permute-start(f32[256]{0:T(256)S(1)} %select_add_fusion.1), channel_id=1, source_target_pairs={{1,2},{2,5},{5,6},{6,9},{9,10},{10,13},{13,14},{14,17},{17,18},{18... | collective-permute-start | bytes 3080 | tf_op jit(solution)/shard_map/ppermute | solution.py:122
  64.0 1.9 %collective-permute-start.4 = (f32[256]{0:T(256)S(1)}, f32[256]{0:T(256)S(1)}, u32[]{:S(2)}, u32[]{:S(2)}) collective-permute-start(f32[256]{0:T(256)S(1)} %select_add_fusion), channel_id=1, source_target_pairs={{1,3},{2,4},{0,1},{3,6},{5,7},{6,8},{4,5},{7,10},{9,11},{10,12},{8... | collective-permute-start | bytes 3080 | tf_op jit(solution)/shard_map/ppermute | solution.py:123
  66.4 3.1 %collective-permute-start.6 = (bf16[256,1152]{1,0:T(8,128)(2,1)S(1)}, bf16[256,1152]{1,0:T(8,128)(2,1)S(1)}, u32[]{:S(2)}, u32[]{:S(2)}) collective-permute-start(bf16[256,1152]{1,0:T(8,128)(2,1)S(1)} %fusion.6), channel_id=1, source_target_pairs={{1,3},{2,4},{0,1},{3,6},{5,7},{6,8},{4,5},{7,10},{9,11},{10,12},{8... | collective-permute-start | bytes 1769480 | tf_op jit(solution)/shard_map/ppermute | solution.py:119
  69.5 10.9 %collective-permute-done.2 = f32[256]{0:T(256)S(1)} collective-permute-done((f32[256]{0:T(256)S(1)}, f32[256]{0:T(256)S(1)}, u32[]{:S(2)}, u32[]{:S(2)}) %collective-permute-start.2) | collective-permute-done | bytes 1056 | tf_op jit(solution)/shard_map/ppermute | solution.py:122
  80.3 0.6 add_multiply_fusion
  80.9 0.6 multiply_reduce_fusion
  81.5 1.3 %subtract_divide_fusion = f32[256,1152]{1,0:T(8,128)} fusion(f32[256,1152]{1,0:T(8,128)S(1)} %get-tuple-element.18, f32[256]{0:T(256)S(1)} %get-tuple-element.17, f32[256]{0:T(256)S(1)} %add_sqrt_fusion.3, bf16[256,1152]{1,0:T(8,128)(2,1)S(1)} %copy-done.1), kind=kLoop, calls=%fused_computation.31 | loop fusion | flops 1474560 | bytes 2951168 | tf_op jit(solution)/shard_map/div | solution.py:51
  82.8 12.0 %collective-permute-done.6 = bf16[256,1152]{1,0:T(8,128)(2,1)S(1)} collective-permute-done((bf16[256,1152]{1,0:T(8,128)(2,1)S(1)}, bf16[256,1152]{1,0:T(8,128)(2,1)S(1)}, u32[]{:S(2)}, u32[]{:S(2)}) %collective-permute-start.6) | collective-permute-done | bytes 589856 | tf_op jit(solution)/shard_map/ppermute | solution.py:119
  94.8 0.5 multiply_reduce_fusion.1
  95.3 1.3 %subtract_divide_fusion.1 = f32[256,1152]{1,0:T(8,128)} fusion(f32[256,1152]{1,0:T(8,128)S(1)} %get-tuple-element.4, f32[256]{0:T(256)S(1)} %get-tuple-element.3, f32[256]{0:T(256)S(1)} %add_sqrt_fusion.4, bf16[256,1152]{1,0:T(8,128)(2,1)S(1)} %copy-done), kind=kLoop, calls=%fused_computation.33 | loop fusion | flops 1474560 | bytes 2951168 | tf_op jit(solution)/shard_map/div | solution.py:51
  (28 shorter events, 4.3 us)
Async XLA Ops:
  0.6 28.8 %copy-start = (bf16[256,1152]{1,0:T(8,128)(2,1)S(1)}, bf16[256,1152]{1,0:T(8,128)(2,1)}, u32[]{:S(2)}) copy-start(bf16[256,1152]{1,0:T(8,128)(2,1)} %param.4) | copy-start | bytes 1769476
  0.6 28.8 %copy-start.1 = (bf16[256,1152]{1,0:T(8,128)(2,1)S(1)}, bf16[256,1152]{1,0:T(8,128)(2,1)}, u32[]{:S(2)}) copy-start(bf16[256,1152]{1,0:T(8,128)(2,1)} %param.5) | copy-start | bytes 1769476
  0.7 30.3 %collective-permute-start.3 = (bf16[256,1152]{1,0:T(8,128)(2,1)}, bf16[256,1152]{1,0:T(8,128)(2,1)S(1)}, u32[]{:S(2)}, u32[]{:S(2)}) collective-permute-start(bf16[256,1152]{1,0:T(8,128)(2,1)} %param.4), channel_id=1, source_target_pairs={{3,1},{4,2},{1,0},{6,3},{7,5},{8,6},{5,4},{10,7},{11,9},{12,10},{9... | collective-permute-start | bytes 1769480 | tf_op jit(solution)/shard_map/ppermute | solution.py:90
  21.7 22.4 %collective-permute-start = (bf16[256,1152]{1,0:T(8,128)(2,1)}, bf16[256,1152]{1,0:T(8,128)(2,1)S(1)}, u32[]{:S(2)}, u32[]{:S(2)}) collective-permute-start(bf16[256,1152]{1,0:T(8,128)(2,1)} %param.4), channel_id=1, source_target_pairs={{2,1},{5,2},{6,5},{9,6},{10,9},{13,10},{14,13},{17,14},{18,17},{21... | collective-permute-start | bytes 1769480 | tf_op jit(solution)/shard_map/ppermute | solution.py:88
  23.7 20.3 %collective-permute-start.1 = (bf16[256,1152]{1,0:T(8,128)(2,1)}, bf16[256,1152]{1,0:T(8,128)(2,1)S(1)}, u32[]{:S(2)}, u32[]{:S(2)}) collective-permute-start(bf16[256,1152]{1,0:T(8,128)(2,1)} %param.5), channel_id=1, source_target_pairs={{0,1},{1,4},{3,2},{2,3},{4,5},{5,8},{7,6},{6,7},{8,9},{9,12},{11,1... | collective-permute-start | bytes 1769480 | tf_op jit(solution)/shard_map/ppermute | solution.py:89
  46.7 34.2 %collective-permute-start.7 = (bf16[256,1152]{1,0:T(8,128)(2,1)S(1)}, bf16[256,1152]{1,0:T(8,128)(2,1)S(1)}, u32[]{:S(2)}, u32[]{:S(2)}) collective-permute-start(bf16[256,1152]{1,0:T(8,128)(2,1)S(1)} %fusion.5), channel_id=1, source_target_pairs={{1,0},{4,1},{2,3},{3,2},{5,4},{8,5},{6,7},{7,6},{9,8},{12,9},{10,1... | collective-permute-start | bytes 1769480 | tf_op jit(solution)/shard_map/ppermute | solution.py:121
  50.4 32.4 %collective-permute-start.5 = (bf16[256,1152]{1,0:T(8,128)(2,1)S(1)}, bf16[256,1152]{1,0:T(8,128)(2,1)S(1)}, u32[]{:S(2)}, u32[]{:S(2)}) collective-permute-start(bf16[256,1152]{1,0:T(8,128)(2,1)S(1)} %get-tuple-element.15), channel_id=1, source_target_pairs={{1,2},{2,5},{5,6},{6,9},{9,10},{10,13},{13,14},{14,17},{17,18},{18... | collective-permute-start | bytes 1769480 | tf_op jit(solution)/shard_map/ppermute | solution.py:111
  62.1 18.3 %collective-permute-start.2 = (f32[256]{0:T(256)S(1)}, f32[256]{0:T(256)S(1)}, u32[]{:S(2)}, u32[]{:S(2)}) collective-permute-start(f32[256]{0:T(256)S(1)} %select_add_fusion.1), channel_id=1, source_target_pairs={{1,2},{2,5},{5,6},{6,9},{9,10},{10,13},{13,14},{14,17},{17,18},{18... | collective-permute-start | bytes 3080 | tf_op jit(solution)/shard_map/ppermute | solution.py:122
  64.0 16.3 %collective-permute-start.4 = (f32[256]{0:T(256)S(1)}, f32[256]{0:T(256)S(1)}, u32[]{:S(2)}, u32[]{:S(2)}) collective-permute-start(f32[256]{0:T(256)S(1)} %select_add_fusion), channel_id=1, source_target_pairs={{1,3},{2,4},{0,1},{3,6},{5,7},{6,8},{4,5},{7,10},{9,11},{10,12},{8... | collective-permute-start | bytes 3080 | tf_op jit(solution)/shard_map/ppermute | solution.py:123
  66.4 28.4 %collective-permute-start.6 = (bf16[256,1152]{1,0:T(8,128)(2,1)S(1)}, bf16[256,1152]{1,0:T(8,128)(2,1)S(1)}, u32[]{:S(2)}, u32[]{:S(2)}) collective-permute-start(bf16[256,1152]{1,0:T(8,128)(2,1)S(1)} %fusion.6), channel_id=1, source_target_pairs={{1,3},{2,4},{0,1},{3,6},{5,7},{6,8},{4,5},{7,10},{9,11},{10,12},{8... | collective-permute-start | bytes 1769480 | tf_op jit(solution)/shard_map/ppermute | solution.py:119

commit v2 on v1

--- a/solution.py
+++ b/solution.py
@@ -5,6 +5,7 @@
 
 HOPS = 4
 GROUP = 4
+RUN = 16
 AXES = ("dp", "group")
 
 
@@ -14,22 +15,18 @@
 
     text, near, far = [], [], []
     for line in range(lines):
-        text += [
-            (at(line, 0), at(line, 1)),
-            (at(line, 1), at(line + 1, 0)),
-            (at(line, 3), at(line, 2)),
-            (at(line, 2), at(line, 3)),
-        ]
-        near += [
-            (at(line, 2), at(line, 1)),
-            (at(line + 1, 1), at(line, 2)),
-        ]
-        far += [
-            (at(line, 3), at(line, 1)),
-            (at(line + 1, 0), at(line, 2)),
-            (at(line, 1), at(line, 0)),
-            (at(line + 1, 2), at(line, 3)),
-        ]
+        text += [(at(line, 0), at(line, 1)), (at(line, 2), at(line, 3))]
+        near += [(at(line, 2), at(line, 1))]
+        far += [(at(line, 3), at(line, 1))]
+        far += [(at(line + 1, 0), at(line, 2))]
+        if line % RUN == RUN - 1:
+            text += [(at(line, 3), at(line + 1, 0)), (at(line, 1), at(line, 2))]
+            near += [(at(line + 1, 0), at(line, 3)), (at(line + 1, 1), at(line + 1, 0))]
+            far += [(at(line + 1, 1), at(line, 3)), (at(line + 1, 2), at(line + 1, 0))]
+        else:
+            text += [(at(line, 1), at(line + 1, 0)), (at(line, 3), at(line, 2))]
+            near += [(at(line + 1, 1), at(line, 2))]
+            far += [(at(line + 1, 1), at(line + 1, 0)), (at(line + 1, 2), at(line, 3))]
     return (text, near, far)
 
 
@@ -80,17 +77,27 @@
 def shards(image_emb, text_emb, scale, bias):
     text_way, near_way, far_way = routes(lax.axis_size("dp"))
     place = lax.axis_index("group")
-    hub = (place == 1) | (place == 2)
+    line = lax.axis_index("dp") % RUN
+    top = line == RUN - 1
+    bottom = line == 0
+    leaf = (place == 0) | (place == 3)
+    top_two = top & (place == 2)
+    hub = ~leaf & ~top_two
+    first = bottom & (place == 0)
+    seam = first | (top & (place == 3))
     s_val = scale[0]
     b_val = bias[0]
     rows = image_emb.shape[0]
 
-    near_raw = lax.ppermute(image_emb, AXES, near_way)
     text_raw = lax.ppermute(text_emb, AXES, text_way)
-    far_raw = lax.ppermute(image_emb, AXES, far_way)
-
     image_unit, image_norm = unit_rows(image_emb)
+    early, image_norm = lax.optimization_barrier((image_emb, image_norm))
+    near_raw = lax.ppermute(early, AXES, near_way)
     text_unit, text_norm = unit_rows(text_emb)
+    late, text_norm = lax.optimization_barrier((early, text_norm))
+    far_raw = lax.ppermute(late, AXES, far_way)
+    image_unit = image_emb.astype(jnp.float32) / image_norm
+    text_unit = text_emb.astype(jnp.float32) / text_norm
     images = image_unit.astype(jnp.bfloat16)
     texts = text_unit.astype(jnp.bfloat16)
     coef, loss = own_terms(images, texts, s_val, b_val)
@@ -98,35 +105,37 @@
     grad_y = columns_by_rows(coef, images)
 
     other = unit_bf(text_raw)
-    near = jnp.where(hub, unit_bf(near_raw), images)
-    far = unit_bf(far_raw)
+    c_ri, l_ri = off_terms(images, other, s_val, b_val, leaf)
+    grad_x = grad_x + jnp.dot(c_ri, other, preferred_element_type=jnp.float32)
 
-    c_on, l_on = off_terms(near, texts, s_val, b_val, hub)
-    c_rn, l_rn = off_terms(near, other, s_val, b_val, True)
+    near = unit_bf(near_raw)
+    c_on, l_on = off_terms(near, texts, s_val, b_val, hub | first)
+    c_rn, l_rn = off_terms(near, other, s_val, b_val, hub | seam)
     grad_near = s_val * (
         jnp.dot(c_on, texts, preferred_element_type=jnp.float32)
         + jnp.dot(c_rn, other, preferred_element_type=jnp.float32)
     )
-    loss_near = l_on + l_rn
     near_back = lax.ppermute(grad_near.astype(jnp.bfloat16), AXES, back(near_way))
+    loss_near_back = lax.ppermute(l_on + l_rn, AXES, back(near_way))
 
-    c_of, l_of = off_terms(far, texts, s_val, b_val, True)
-    c_rf, l_rf = off_terms(far, other, s_val, b_val, hub)
+    far = unit_bf(far_raw)
+    c_of, l_of = off_terms(far, texts, s_val, b_val, hub | (leaf & ~seam))
+    c_rf, l_rf = off_terms(far, other, s_val, b_val, hub | seam | top_two)
     grad_far = s_val * (
         jnp.dot(c_of, texts, preferred_element_type=jnp.float32)
         + jnp.dot(c_rf, other, preferred_element_type=jnp.float32)
     )
     far_back = lax.ppermute(grad_far.astype(jnp.bfloat16), AXES, back(far_way))
-    grad_other = s_val * (columns_by_rows(c_rn, near) + columns_by_rows(c_rf, far))
+    grad_other = s_val * (
+        columns_by_rows(c_ri, images) + columns_by_rows(c_rn, near) + columns_by_rows(c_rf, far)
+    )
     text_back = lax.ppermute(grad_other.astype(jnp.bfloat16), AXES, back(text_way))
-    loss_near_back = lax.ppermute(loss_near, AXES, back(near_way))
     loss_far_back = lax.ppermute(l_of + l_rf, AXES, back(far_way))
 
     grad_y = s_val * (grad_y + columns_by_rows(c_on, near) + columns_by_rows(c_of, far))
     grad_y = grad_y + text_back.astype(jnp.float32)
-    grad_x = s_val * grad_x + jnp.where(hub, near_back.astype(jnp.float32), grad_near)
-    grad_x = grad_x + far_back.astype(jnp.float32)
-    loss = loss + jnp.where(hub, loss_near_back, loss_near) + loss_far_back
+    grad_x = s_val * grad_x + near_back.astype(jnp.float32) + far_back.astype(jnp.float32)
+    loss = loss + l_ri + loss_near_back + loss_far_back
     row_loss = loss / (HOPS * rows)
     grad_image = back_norm(grad_x, image_unit, image_norm)
     grad_text = back_norm(grad_y, text_unit, text_norm)

time: 97 us -> 88.7 us (0.914)
  the two profiles are of different devices: /device:TPU:128 before, /device:TPU:770 now
where the time goes in v2:
time: 88.7 us; the launch traced here: 88.2 us
  waiting for transfers between devices  42.1 us (47%)
  starting transfers between devices  26.4 us (30%)
  matrix products  11 us (12%)
  other arithmetic  6.54 us (7%)
  between operations  2.12 us (2%)
    ppermute x1, waiting for transfers between devices, shards(): far_raw = lax.ppermute(late, AXES, far_way)  11.5 us
    ppermute x1, waiting for transfers between devices, shards(): loss_near_back = lax.ppermute(l_on + l_rn, AXES, back(near_way))  11.4 us
    ppermute x1, waiting for transfers between devices, shards(): near_raw = lax.ppermute(early, AXES, near_way)  10.6 us
    ppermute x1, waiting for transfers between devices, shards(): loss_far_back = lax.ppermute(l_of + l_rf, AXES, back(far_way))  8.63 us
    ppermute x1, starting transfers between devices, shards(): lax.ppermute(grad_other.astype(jnp.bfloat16), AXES, back(text_way))  7.23 us
    ppermute x1, starting transfers between devices, shards(): near_raw = lax.ppermute(early, AXES, near_way)  5.5 us
    dot_general x6, matrix products, rows_by_rows(): lax.dot_general(a, b, (((1,), (1,)), ((), ())), preferred_element_type=jn...  4.29 us
    dot_general x6, matrix products, columns_by_rows(): lax.dot_general(a, b, (((0,), (0,)), ((), ())), preferred_element_type=jn...  3.9 us
  transfers between devices with their start and end apart: 8, of which 4 were waited for; matrix products, arithmetic and copies ran while one was open for 15% of the time, Pallas kernels for 0%

profile of v2, /device:TPU:770, one launch (start us, length us, event | category | flops | bytes accessed | tf_op | source)
XLA Modules:
  0.0 88.2 jit_solution(16363631289879791386)
XLA Ops:
  0.7 3.5 %collective-permute-start = (bf16[256,1152]{1,0:T(8,128)(2,1)}, bf16[256,1152]{1,0:T(8,128)(2,1)S(1)}, u32[]{:S(2)}, u32[]{:S(2)}) collective-permute-start(bf16[256,1152]{1,0:T(8,128)(2,1)} %param.5), channel_id=1, source_target_pairs={{0,1},{2,3},{1,4},{3,2},{4,5},{6,7},{5,8},{7,6},{8,9},{10,11},{9,1... | collective-permute-start | bytes 1769480 | tf_op jit(solution)/shard_map/ppermute | solution.py:92
  4.2 1.3 %fusion.11 = f32[256]{0:T(256)S(1)} fusion(bf16[256,1152]{1,0:T(8,128)(2,1)} %param.4), kind=kLoop, calls=%fused_computation.28 | loop fusion | flops 884480 | bytes 590848 | tf_op jit(solution)/shard_map/reduce_sum | solution.py:39
  5.4 5.5 %collective-permute-start.1 = (bf16[256,1152]{1,0:T(8,128)(2,1)}, bf16[256,1152]{1,0:T(8,128)(2,1)S(1)}, u32[]{:S(2)}, u32[]{:S(2)}) collective-permute-start(bf16[256,1152]{1,0:T(8,128)(2,1)} %param.4), channel_id=1, source_target_pairs={{2,1},{5,2},{6,5},{9,6},{10,9},{13,10},{14,13},{17,14},{18,17},{21... | collective-permute-start | bytes 1769480 | tf_op jit(solution)/shard_map/ppermute | solution.py:95
  11.0 1.3 %fusion.12 = f32[256]{0:T(256)S(1)} fusion(bf16[256,1152]{1,0:T(8,128)(2,1)} %param.5), kind=kLoop, calls=%fused_computation.29 | loop fusion | flops 884480 | bytes 590848 | tf_op jit(solution)/shard_map/reduce_sum | solution.py:39
  12.2 2.4 %collective-permute-start.3 = (bf16[256,1152]{1,0:T(8,128)(2,1)S(1)}, bf16[256,1152]{1,0:T(8,128)(2,1)S(1)}, u32[]{:S(2)}, u32[]{:S(2)}) collective-permute-start(bf16[256,1152]{1,0:T(8,128)(2,1)S(1)} %copy-done.1), channel_id=1, source_target_pairs={{3,1},{4,2},{5,4},{6,3},{7,5},{8,6},{9,8},{10,7},{11,9},{12,10},{1... | collective-permute-start | bytes 1769480 | tf_op jit(solution)/shard_map/ppermute | solution.py:98
  16.2 1.3 %fusion.26 = (f32[256]{0:T(256)S(1)}, f32[256,256]{0,1:T(8,128)}) fusion(f32[]{:T(128)} %bitcast.23, bf16[256,1152]{1,0:T(8,128)(2,1)S(1)} %fusion.51, f32[256]{0:T(256)S(1)} %add_sqrt_fusion.4, bf16[256,1152]{1,0:T(8,128)(2,1)S(1)} %copy-done.1, f32[]{:T(128)} %bitcast.12), kind=kOutput, calls=%fused_computation.59 | convolution fusion | flops 152731392 | bytes 1443848 | tf_op jit(solution)/shard_map/dot_general | solution.py:52
  17.5 1.5 %fusion.52 = f32[256,1152]{1,0:T(8,128)S(1)} fusion(f32[256,256]{0,1:T(8,128)} %get-tuple-element.20, f32[256]{0:T(256)S(1)} %add_sqrt_fusion.4, bf16[256,1152]{1,0:T(8,128)(2,1)S(1)} %copy-done.1), kind=kOutput, calls=%fused_computation.91 | convolution fusion | flops 152403968 | bytes 2032640 | tf_op jit(solution)/shard_map/dot_general | solution.py:56
  19.6 10.6 %collective-permute-done.1 = bf16[256,1152]{1,0:T(8,128)(2,1)S(1)} collective-permute-done((bf16[256,1152]{1,0:T(8,128)(2,1)}, bf16[256,1152]{1,0:T(8,128)(2,1)S(1)}, u32[]{:S(2)}, u32[]{:S(2)}) %collective-permute-start.1) | collective-permute-done | bytes 589856 | tf_op jit(solution)/shard_map/ppermute | solution.py:95
  30.4 0.6 fusion.27
  31.5 11.5 %collective-permute-done.3 = bf16[256,1152]{1,0:T(8,128)(2,1)S(1)} collective-permute-done((bf16[256,1152]{1,0:T(8,128)(2,1)S(1)}, bf16[256,1152]{1,0:T(8,128)(2,1)S(1)}, u32[]{:S(2)}, u32[]{:S(2)}) %collective-permute-start.3) | collective-permute-done | bytes 589856 | tf_op jit(solution)/shard_map/ppermute | solution.py:98
  43.2 0.6 fusion.29
  44.3 0.6 fusion.31
  45.3 7.2 %collective-permute-start.7 = (bf16[256,1152]{1,0:T(8,128)(2,1)S(1)}, bf16[256,1152]{1,0:T(8,128)(2,1)S(1)}, u32[]{:S(2)}, u32[]{:S(2)}) collective-permute-start(bf16[256,1152]{1,0:T(8,128)(2,1)S(1)} %fusion.8), channel_id=1, source_target_pairs={{1,0},{3,2},{4,1},{2,3},{5,4},{7,6},{8,5},{6,7},{9,8},{11,10},{12,... | collective-permute-start | bytes 1769480 | tf_op jit(solution)/shard_map/ppermute | solution.py:132
  52.6 0.6 fusion.28
  54.0 1.9 %collective-permute-start.5 = (bf16[256,1152]{1,0:T(8,128)(2,1)S(1)}, bf16[256,1152]{1,0:T(8,128)(2,1)S(1)}, u32[]{:S(2)}, u32[]{:S(2)}) collective-permute-start(bf16[256,1152]{1,0:T(8,128)(2,1)S(1)} %fusion.10), channel_id=1, source_target_pairs={{1,2},{2,5},{5,6},{6,9},{9,10},{10,13},{13,14},{14,17},{17,18},{18... | collective-permute-start | bytes 1769480 | tf_op jit(solution)/shard_map/ppermute | solution.py:118
  57.4 1.9 %collective-permute-start.6 = (bf16[256,1152]{1,0:T(8,128)(2,1)S(1)}, bf16[256,1152]{1,0:T(8,128)(2,1)S(1)}, u32[]{:S(2)}, u32[]{:S(2)}) collective-permute-start(bf16[256,1152]{1,0:T(8,128)(2,1)S(1)} %fusion.9), channel_id=1, source_target_pairs={{1,3},{2,4},{4,5},{3,6},{5,7},{6,8},{8,9},{7,10},{9,11},{10,12},{1... | collective-permute-start | bytes 1769480 | tf_op jit(solution)/shard_map/ppermute | solution.py:128
  59.3 1.9 %collective-permute-start.2 = (f32[256]{0:T(256)S(1)}, f32[256]{0:T(256)S(1)}, u32[]{:S(2)}, u32[]{:S(2)}) collective-permute-start(f32[256]{0:T(256)S(1)} %select_add_fusion.1), channel_id=1, source_target_pairs={{1,2},{2,5},{5,6},{6,9},{9,10},{10,13},{13,14},{14,17},{17,18},{18... | collective-permute-start | bytes 3080 | tf_op jit(solution)/shard_map/ppermute | solution.py:119
  61.3 1.9 %collective-permute-start.4 = (f32[256]{0:T(256)S(1)}, f32[256]{0:T(256)S(1)}, u32[]{:S(2)}, u32[]{:S(2)}) collective-permute-start(f32[256]{0:T(256)S(1)} %select_add_fusion), channel_id=1, source_target_pairs={{1,3},{2,4},{4,5},{3,6},{5,7},{6,8},{8,9},{7,10},{9,11},{10,12},{1... | collective-permute-start | bytes 3080 | tf_op jit(solution)/shard_map/ppermute | solution.py:133
  63.6 11.4 %collective-permute-done.2 = f32[256]{0:T(256)S(1)} collective-permute-done((f32[256]{0:T(256)S(1)}, f32[256]{0:T(256)S(1)}, u32[]{:S(2)}, u32[]{:S(2)}) %collective-permute-start.2) | collective-permute-done | bytes 1056 | tf_op jit(solution)/shard_map/ppermute | solution.py:119
  75.0 8.6 %collective-permute-done.4 = f32[256]{0:T(256)S(1)} collective-permute-done((f32[256]{0:T(256)S(1)}, f32[256]{0:T(256)S(1)}, u32[]{:S(2)}, u32[]{:S(2)}) %collective-permute-start.4) | collective-permute-done | bytes 1056 | tf_op jit(solution)/shard_map/ppermute | solution.py:133
  84.2 0.7 multiply_reduce_fusion
  84.9 1.3 %subtract_divide_fusion = f32[256,1152]{1,0:T(8,128)} fusion(f32[256,1152]{1,0:T(8,128)S(1)} %get-tuple-element.26, f32[256]{0:T(256)S(1)} %get-tuple-element.25, f32[256]{0:T(256)S(1)} %add_sqrt_fusion.3, bf16[256,1152]{1,0:T(8,128)(2,1)S(1)} %copy-done), kind=kLoop, calls=%fused_computation.36 | loop fusion | flops 1474560 | bytes 2951168 | tf_op jit(solution)/shard_map/div | solution.py:48
  86.2 0.7 multiply_reduce_fusion.1
  86.9 1.3 %subtract_divide_fusion.1 = f32[256,1152]{1,0:T(8,128)} fusion(f32[256,1152]{1,0:T(8,128)S(1)} %get-tuple-element.24, f32[256]{0:T(256)S(1)} %get-tuple-element.23, f32[256]{0:T(256)S(1)} %add_sqrt_fusion.4, bf16[256,1152]{1,0:T(8,128)(2,1)S(1)} %copy-done.1), kind=kLoop, calls=%fused_computation.38 | loop fusion | flops 1474560 | bytes 2951168 | tf_op jit(solution)/shard_map/div | solution.py:48
  (32 shorter events, 5.9 us)
Async XLA Ops:
  0.6 15.4 %copy-start = (bf16[256,1152]{1,0:T(8,128)(2,1)S(1)}, bf16[256,1152]{1,0:T(8,128)(2,1)}, u32[]{:S(2)}) copy-start(bf16[256,1152]{1,0:T(8,128)(2,1)} %param.5) | copy-start | bytes 1769476
  0.6 11.6 %copy-start.1 = (bf16[256,1152]{1,0:T(8,128)(2,1)S(1)}, bf16[256,1152]{1,0:T(8,128)(2,1)}, u32[]{:S(2)}) copy-start(bf16[256,1152]{1,0:T(8,128)(2,1)} %param.4) | copy-start | bytes 1769476
  0.7 18.8 %collective-permute-start = (bf16[256,1152]{1,0:T(8,128)(2,1)}, bf16[256,1152]{1,0:T(8,128)(2,1)S(1)}, u32[]{:S(2)}, u32[]{:S(2)}) collective-permute-start(bf16[256,1152]{1,0:T(8,128)(2,1)} %param.5), channel_id=1, source_target_pairs={{0,1},{2,3},{1,4},{3,2},{4,5},{6,7},{5,8},{7,6},{8,9},{10,11},{9,1... | collective-permute-start | bytes 1769480 | tf_op jit(solution)/shard_map/ppermute | solution.py:92
  5.4 24.8 %collective-permute-start.1 = (bf16[256,1152]{1,0:T(8,128)(2,1)}, bf16[256,1152]{1,0:T(8,128)(2,1)S(1)}, u32[]{:S(2)}, u32[]{:S(2)}) collective-permute-start(bf16[256,1152]{1,0:T(8,128)(2,1)} %param.4), channel_id=1, source_target_pairs={{2,1},{5,2},{6,5},{9,6},{10,9},{13,10},{14,13},{17,14},{18,17},{21... | collective-permute-start | bytes 1769480 | tf_op jit(solution)/shard_map/ppermute | solution.py:95
  12.2 30.8 %collective-permute-start.3 = (bf16[256,1152]{1,0:T(8,128)(2,1)S(1)}, bf16[256,1152]{1,0:T(8,128)(2,1)S(1)}, u32[]{:S(2)}, u32[]{:S(2)}) collective-permute-start(bf16[256,1152]{1,0:T(8,128)(2,1)S(1)} %copy-done.1), channel_id=1, source_target_pairs={{3,1},{4,2},{5,4},{6,3},{7,5},{8,6},{9,8},{10,7},{11,9},{12,10},{1... | collective-permute-start | bytes 1769480 | tf_op jit(solution)/shard_map/ppermute | solution.py:98
  17.5 1.5 %copy-start.2 = (f32[256,256]{0,1:T(8,128)S(1)}, f32[256,256]{0,1:T(8,128)}, u32[]{:S(2)}) copy-start(f32[256,256]{0,1:T(8,128)} %get-tuple-element.20) | copy-start | bytes 786436
  45.3 38.9 %collective-permute-start.7 = (bf16[256,1152]{1,0:T(8,128)(2,1)S(1)}, bf16[256,1152]{1,0:T(8,128)(2,1)S(1)}, u32[]{:S(2)}, u32[]{:S(2)}) collective-permute-start(bf16[256,1152]{1,0:T(8,128)(2,1)S(1)} %fusion.8), channel_id=1, source_target_pairs={{1,0},{3,2},{4,1},{2,3},{5,4},{7,6},{8,5},{6,7},{9,8},{11,10},{12,... | collective-permute-start | bytes 1769480 | tf_op jit(solution)/shard_map/ppermute | solution.py:132
  54.0 32.2 %collective-permute-start.5 = (bf16[256,1152]{1,0:T(8,128)(2,1)S(1)}, bf16[256,1152]{1,0:T(8,128)(2,1)S(1)}, u32[]{:S(2)}, u32[]{:S(2)}) collective-permute-start(bf16[256,1152]{1,0:T(8,128)(2,1)S(1)} %fusion.10), channel_id=1, source_target_pairs={{1,2},{2,5},{5,6},{6,9},{9,10},{10,13},{13,14},{14,17},{17,18},{18... | collective-permute-start | bytes 1769480 | tf_op jit(solution)/shard_map/ppermute | solution.py:118
  57.4 28.8 %collective-permute-start.6 = (bf16[256,1152]{1,0:T(8,128)(2,1)S(1)}, bf16[256,1152]{1,0:T(8,128)(2,1)S(1)}, u32[]{:S(2)}, u32[]{:S(2)}) collective-permute-start(bf16[256,1152]{1,0:T(8,128)(2,1)S(1)} %fusion.9), channel_id=1, source_target_pairs={{1,3},{2,4},{4,5},{3,6},{5,7},{6,8},{8,9},{7,10},{9,11},{10,12},{1... | collective-permute-start | bytes 1769480 | tf_op jit(solution)/shard_map/ppermute | solution.py:128
  59.3 15.7 %collective-permute-start.2 = (f32[256]{0:T(256)S(1)}, f32[256]{0:T(256)S(1)}, u32[]{:S(2)}, u32[]{:S(2)}) collective-permute-start(f32[256]{0:T(256)S(1)} %select_add_fusion.1), channel_id=1, source_target_pairs={{1,2},{2,5},{5,6},{6,9},{9,10},{10,13},{13,14},{14,17},{17,18},{18... | collective-permute-start | bytes 3080 | tf_op jit(solution)/shard_map/ppermute | solution.py:119
  61.3 22.4 %collective-permute-start.4 = (f32[256]{0:T(256)S(1)}, f32[256]{0:T(256)S(1)}, u32[]{:S(2)}, u32[]{:S(2)}) collective-permute-start(f32[256]{0:T(256)S(1)} %select_add_fusion), channel_id=1, source_target_pairs={{1,3},{2,4},{4,5},{3,6},{5,7},{6,8},{8,9},{7,10},{9,11},{10,12},{1... | collective-permute-start | bytes 3080 | tf_op jit(solution)/shard_map/ppermute | solution.py:133

commit v3 on v2

--- a/solution.py
+++ b/solution.py
@@ -116,7 +116,6 @@
         + jnp.dot(c_rn, other, preferred_element_type=jnp.float32)
     )
     near_back = lax.ppermute(grad_near.astype(jnp.bfloat16), AXES, back(near_way))
-    loss_near_back = lax.ppermute(l_on + l_rn, AXES, back(near_way))
 
     far = unit_bf(far_raw)
     c_of, l_of = off_terms(far, texts, s_val, b_val, hub | (leaf & ~seam))
@@ -130,9 +129,11 @@
         columns_by_rows(c_ri, images) + columns_by_rows(c_rn, near) + columns_by_rows(c_rf, far)
     )
     text_back = lax.ppermute(grad_other.astype(jnp.bfloat16), AXES, back(text_way))
-    loss_far_back = lax.ppermute(l_of + l_rf, AXES, back(far_way))
 
     grad_y = s_val * (grad_y + columns_by_rows(c_on, near) + columns_by_rows(c_of, far))
+    grad_y, loss_near, loss_far = lax.optimization_barrier((grad_y, l_on + l_rn, l_of + l_rf))
+    loss_near_back = lax.ppermute(loss_near, AXES, back(near_way))
+    loss_far_back = lax.ppermute(loss_far, AXES, back(far_way))
     grad_y = grad_y + text_back.astype(jnp.float32)
     grad_x = s_val * grad_x + near_back.astype(jnp.float32) + far_back.astype(jnp.float32)
     loss = loss + l_ri + loss_near_back + loss_far_back

time: 88.7 us -> 87.1 us (0.982)
  the two profiles are of different devices: /device:TPU:770 before, /device:TPU:6 now
where the time goes in v3:
time: 87.1 us; the launch traced here: 86.6 us
  starting transfers between devices  41.8 us (48%)
  waiting for transfers between devices  24.9 us (29%)
  matrix products  10.8 us (12%)
  other arithmetic  7 us (8%)
  between operations  2.13 us (2%)
    ppermute x1, starting transfers between devices, shards(): near_raw = lax.ppermute(early, AXES, near_way)  18.5 us
    ppermute x1, waiting for transfers between devices, shards(): loss_far_back = lax.ppermute(loss_far, AXES, back(far_way))  10.4 us
    ppermute x1, waiting for transfers between devices, shards(): far_raw = lax.ppermute(late, AXES, far_way)  9.89 us
    ppermute x1, starting transfers between devices, shards(): lax.ppermute(grad_other.astype(jnp.bfloat16), AXES, back(text_way))  7.79 us
    ppermute x1, waiting for transfers between devices, shards(): loss_near_back = lax.ppermute(loss_near, AXES, back(near_way))  4.55 us
    ppermute x1, starting transfers between devices, shards(): text_raw = lax.ppermute(text_emb, AXES, text_way)  4.41 us
    dot_general x6, matrix products, rows_by_rows(): lax.dot_general(a, b, (((1,), (1,)), ((), ())), preferred_element_type=jn...  4.31 us
    dot_general x6, matrix products, columns_by_rows(): lax.dot_general(a, b, (((0,), (0,)), ((), ())), preferred_element_type=jn...  3.67 us
  transfers between devices with their start and end apart: 8, of which 3 were waited for; matrix products, arithmetic and copies ran while one was open for 13% of the time, Pallas kernels for 0%

profile of v3, /device:TPU:6, one launch (start us, length us, event | category | flops | bytes accessed | tf_op | source)
XLA Modules:
  0.0 86.6 jit_solution(7228223497110569030)
XLA Ops:
  0.7 4.4 %collective-permute-start = (bf16[256,1152]{1,0:T(8,128)(2,1)}, bf16[256,1152]{1,0:T(8,128)(2,1)S(1)}, u32[]{:S(2)}, u32[]{:S(2)}) collective-permute-start(bf16[256,1152]{1,0:T(8,128)(2,1)} %param.5), channel_id=1, source_target_pairs={{0,1},{2,3},{1,4},{3,2},{4,5},{6,7},{5,8},{7,6},{8,9},{10,11},{9,1... | collective-permute-start | bytes 1769480 | tf_op jit(solution)/shard_map/ppermute | solution.py:92
  5.1 1.3 %fusion.10 = f32[256]{0:T(256)S(1)} fusion(bf16[256,1152]{1,0:T(8,128)(2,1)} %param.4), kind=kLoop, calls=%fused_computation.27 | loop fusion | flops 884480 | bytes 590848 | tf_op jit(solution)/shard_map/reduce_sum | solution.py:39
  6.3 18.5 %collective-permute-start.1 = (bf16[256,1152]{1,0:T(8,128)(2,1)}, bf16[256,1152]{1,0:T(8,128)(2,1)S(1)}, u32[]{:S(2)}, u32[]{:S(2)}) collective-permute-start(bf16[256,1152]{1,0:T(8,128)(2,1)} %param.4), channel_id=1, source_target_pairs={{2,1},{5,2},{6,5},{9,6},{10,9},{13,10},{14,13},{17,14},{18,17},{21... | collective-permute-start | bytes 1769480 | tf_op jit(solution)/shard_map/ppermute | solution.py:95
  24.8 1.3 %fusion.11 = f32[256]{0:T(256)S(1)} fusion(bf16[256,1152]{1,0:T(8,128)(2,1)} %param.5), kind=kLoop, calls=%fused_computation.28 | loop fusion | flops 884480 | bytes 590848 | tf_op jit(solution)/shard_map/reduce_sum | solution.py:39
  26.1 3.4 %collective-permute-start.2 = (bf16[256,1152]{1,0:T(8,128)(2,1)S(1)}, bf16[256,1152]{1,0:T(8,128)(2,1)S(1)}, u32[]{:S(2)}, u32[]{:S(2)}) collective-permute-start(bf16[256,1152]{1,0:T(8,128)(2,1)S(1)} %copy-done.1), channel_id=1, source_target_pairs={{3,1},{4,2},{5,4},{6,3},{7,5},{8,6},{9,8},{10,7},{11,9},{12,10},{1... | collective-permute-start | bytes 1769480 | tf_op jit(solution)/shard_map/ppermute | solution.py:98
  31.0 1.3 %fusion.25 = (f32[256]{0:T(256)S(1)}, f32[256,256]{0,1:T(8,128)}) fusion(f32[]{:T(128)} %bitcast.23, bf16[256,1152]{1,0:T(8,128)(2,1)S(1)} %fusion.50, f32[256]{0:T(256)S(1)} %add_sqrt_fusion.4, bf16[256,1152]{1,0:T(8,128)(2,1)S(1)} %copy-done.1, f32[]{:T(128)} %bitcast.12), kind=kOutput, calls=%fused_computation.59 | convolution fusion | flops 152731392 | bytes 1443848 | tf_op jit(solution)/shard_map/dot_general | solution.py:52
  32.3 1.5 %fusion.52 = f32[256,1152]{1,0:T(8,128)S(1)} fusion(f32[256,256]{0,1:T(8,128)} %get-tuple-element.26, f32[256]{0:T(256)S(1)} %add_sqrt_fusion.4, bf16[256,1152]{1,0:T(8,128)(2,1)S(1)} %copy-done.1), kind=kOutput, calls=%fused_computation.92 | convolution fusion | flops 152403968 | bytes 2032640 | tf_op jit(solution)/shard_map/dot_general | solution.py:56
  34.7 0.6 fusion.26
  35.7 9.9 %collective-permute-done.2 = bf16[256,1152]{1,0:T(8,128)(2,1)S(1)} collective-permute-done((bf16[256,1152]{1,0:T(8,128)(2,1)S(1)}, bf16[256,1152]{1,0:T(8,128)(2,1)S(1)}, u32[]{:S(2)}, u32[]{:S(2)}) %collective-permute-start.2) | collective-permute-done | bytes 589856 | tf_op jit(solution)/shard_map/ppermute | solution.py:98
  45.8 0.6 fusion.27
  46.8 0.6 fusion.28
  47.5 0.6 fusion.29
  48.5 0.6 fusion.30
  50.4 1.9 %collective-permute-start.6 = (bf16[256,1152]{1,0:T(8,128)(2,1)S(1)}, bf16[256,1152]{1,0:T(8,128)(2,1)S(1)}, u32[]{:S(2)}, u32[]{:S(2)}) collective-permute-start(bf16[256,1152]{1,0:T(8,128)(2,1)S(1)} %fusion.8), channel_id=1, source_target_pairs={{1,3},{2,4},{4,5},{3,6},{5,7},{6,8},{8,9},{7,10},{9,11},{10,12},{1... | collective-permute-start | bytes 1769480 | tf_op jit(solution)/shard_map/ppermute | solution.py:127
  52.8 1.9 %collective-permute-start.5 = (bf16[256,1152]{1,0:T(8,128)(2,1)S(1)}, bf16[256,1152]{1,0:T(8,128)(2,1)S(1)}, u32[]{:S(2)}, u32[]{:S(2)}) collective-permute-start(bf16[256,1152]{1,0:T(8,128)(2,1)S(1)} %fusion.9), channel_id=1, source_target_pairs={{1,2},{2,5},{5,6},{6,9},{9,10},{10,13},{13,14},{14,17},{17,18},{18... | collective-permute-start | bytes 1769480 | tf_op jit(solution)/shard_map/ppermute | solution.py:118
  54.7 2.0 %collective-permute-start.3 = (f32[256]{0:T(256)S(1)}, f32[256]{0:T(256)S(1)}, u32[]{:S(2)}, u32[]{:S(2)}) collective-permute-start(f32[256]{0:T(256)S(1)} %select_add_fusion.1), channel_id=1, source_target_pairs={{1,2},{2,5},{5,6},{6,9},{9,10},{10,13},{13,14},{14,17},{17,18},{18... | collective-permute-start | bytes 3080 | tf_op jit(solution)/shard_map/ppermute | solution.py:135
  56.7 1.9 %collective-permute-start.4 = (f32[256]{0:T(256)S(1)}, f32[256]{0:T(256)S(1)}, u32[]{:S(2)}, u32[]{:S(2)}) collective-permute-start(f32[256]{0:T(256)S(1)} %select_add_fusion), channel_id=1, source_target_pairs={{1,3},{2,4},{4,5},{3,6},{5,7},{6,8},{8,9},{7,10},{9,11},{10,12},{1... | collective-permute-start | bytes 3080 | tf_op jit(solution)/shard_map/ppermute | solution.py:136
  59.5 7.8 %collective-permute-start.7 = (bf16[256,1152]{1,0:T(8,128)(2,1)S(1)}, bf16[256,1152]{1,0:T(8,128)(2,1)S(1)}, u32[]{:S(2)}, u32[]{:S(2)}) collective-permute-start(bf16[256,1152]{1,0:T(8,128)(2,1)S(1)} %fusion.7), channel_id=1, source_target_pairs={{1,0},{3,2},{4,1},{2,3},{5,4},{7,6},{8,5},{6,7},{9,8},{11,10},{12,... | collective-permute-start | bytes 1769480 | tf_op jit(solution)/shard_map/ppermute | solution.py:131
  67.3 4.5 %collective-permute-done.3 = f32[256]{0:T(256)S(1)} collective-permute-done((f32[256]{0:T(256)S(1)}, f32[256]{0:T(256)S(1)}, u32[]{:S(2)}, u32[]{:S(2)}) %collective-permute-start.3) | collective-permute-done | bytes 1056 | tf_op jit(solution)/shard_map/ppermute | solution.py:135
  71.9 10.4 %collective-permute-done.4 = f32[256]{0:T(256)S(1)} collective-permute-done((f32[256]{0:T(256)S(1)}, f32[256]{0:T(256)S(1)}, u32[]{:S(2)}, u32[]{:S(2)}) %collective-permute-start.4) | collective-permute-done | bytes 1056 | tf_op jit(solution)/shard_map/ppermute | solution.py:136
  82.3 0.6 add_multiply_fusion
  82.8 0.7 multiply_reduce_fusion.1
  83.6 1.3 %subtract_divide_fusion.1 = f32[256,1152]{1,0:T(8,128)} fusion(f32[256,1152]{1,0:T(8,128)S(1)} %get-tuple-element.30, f32[256]{0:T(256)S(1)} %get-tuple-element.29, f32[256]{0:T(256)S(1)} %add_sqrt_fusion.4, bf16[256,1152]{1,0:T(8,128)(2,1)S(1)} %copy-done.1), kind=kLoop, calls=%fused_computation.38 | loop fusion | flops 1474560 | bytes 2951168 | tf_op jit(solution)/shard_map/div | solution.py:48
  85.3 1.4 %subtract_divide_fusion = f32[256,1152]{1,0:T(8,128)} fusion(f32[256,1152]{1,0:T(8,128)S(1)} %fusion, bf16[256,1152]{1,0:T(8,128)(2,1)S(1)} %collective-permute-done.7, f32[256]{0:T(256)S(1)} %multiply_reduce_fusion, f32[256]{0:T(256)S(1)} %add_sqrt_fusion.3, bf16[256,1152]{1,0:T(8,128)(2,1)S(1)} %copy-done), kind=kLoop, calls=%fused_computation.35 | loop fusion | flops 2064384 | bytes 3540992 | tf_op jit(solution)/shard_map/div | solution.py:48
  (33 shorter events, 5.6 us)
Async XLA Ops:
  0.6 30.2 %copy-start = (bf16[256,1152]{1,0:T(8,128)(2,1)S(1)}, bf16[256,1152]{1,0:T(8,128)(2,1)}, u32[]{:S(2)}) copy-start(bf16[256,1152]{1,0:T(8,128)(2,1)} %param.5) | copy-start | bytes 1769476
  0.6 25.5 %copy-start.1 = (bf16[256,1152]{1,0:T(8,128)(2,1)S(1)}, bf16[256,1152]{1,0:T(8,128)(2,1)}, u32[]{:S(2)}) copy-start(bf16[256,1152]{1,0:T(8,128)(2,1)} %param.4) | copy-start | bytes 1769476
  0.7 33.6 %collective-permute-start = (bf16[256,1152]{1,0:T(8,128)(2,1)}, bf16[256,1152]{1,0:T(8,128)(2,1)S(1)}, u32[]{:S(2)}, u32[]{:S(2)}) collective-permute-start(bf16[256,1152]{1,0:T(8,128)(2,1)} %param.5), channel_id=1, source_target_pairs={{0,1},{2,3},{1,4},{3,2},{4,5},{6,7},{5,8},{7,6},{8,9},{10,11},{9,1... | collective-permute-start | bytes 1769480 | tf_op jit(solution)/shard_map/ppermute | solution.py:92
  6.3 28.1 %collective-permute-start.1 = (bf16[256,1152]{1,0:T(8,128)(2,1)}, bf16[256,1152]{1,0:T(8,128)(2,1)S(1)}, u32[]{:S(2)}, u32[]{:S(2)}) collective-permute-start(bf16[256,1152]{1,0:T(8,128)(2,1)} %param.4), channel_id=1, source_target_pairs={{2,1},{5,2},{6,5},{9,6},{10,9},{13,10},{14,13},{17,14},{18,17},{21... | collective-permute-start | bytes 1769480 | tf_op jit(solution)/shard_map/ppermute | solution.py:95
  26.1 19.5 %collective-permute-start.2 = (bf16[256,1152]{1,0:T(8,128)(2,1)S(1)}, bf16[256,1152]{1,0:T(8,128)(2,1)S(1)}, u32[]{:S(2)}, u32[]{:S(2)}) collective-permute-start(bf16[256,1152]{1,0:T(8,128)(2,1)S(1)} %copy-done.1), channel_id=1, source_target_pairs={{3,1},{4,2},{5,4},{6,3},{7,5},{8,6},{9,8},{10,7},{11,9},{12,10},{1... | collective-permute-start | bytes 1769480 | tf_op jit(solution)/shard_map/ppermute | solution.py:98
  32.3 1.5 %copy-start.2 = (f32[256,256]{0,1:T(8,128)S(1)}, f32[256,256]{0,1:T(8,128)}, u32[]{:S(2)}) copy-start(f32[256,256]{0,1:T(8,128)} %get-tuple-element.26) | copy-start | bytes 786436
  50.4 32.4 %collective-permute-start.6 = (bf16[256,1152]{1,0:T(8,128)(2,1)S(1)}, bf16[256,1152]{1,0:T(8,128)(2,1)S(1)}, u32[]{:S(2)}, u32[]{:S(2)}) collective-permute-start(bf16[256,1152]{1,0:T(8,128)(2,1)S(1)} %fusion.8), channel_id=1, source_target_pairs={{1,3},{2,4},{4,5},{3,6},{5,7},{6,8},{8,9},{7,10},{9,11},{10,12},{1... | collective-permute-start | bytes 1769480 | tf_op jit(solution)/shard_map/ppermute | solution.py:127
  52.8 30.1 %collective-permute-start.5 = (bf16[256,1152]{1,0:T(8,128)(2,1)S(1)}, bf16[256,1152]{1,0:T(8,128)(2,1)S(1)}, u32[]{:S(2)}, u32[]{:S(2)}) collective-permute-start(bf16[256,1152]{1,0:T(8,128)(2,1)S(1)} %fusion.9), channel_id=1, source_target_pairs={{1,2},{2,5},{5,6},{6,9},{9,10},{10,13},{13,14},{14,17},{17,18},{18... | collective-permute-start | bytes 1769480 | tf_op jit(solution)/shard_map/ppermute | solution.py:118
  54.7 17.2 %collective-permute-start.3 = (f32[256]{0:T(256)S(1)}, f32[256]{0:T(256)S(1)}, u32[]{:S(2)}, u32[]{:S(2)}) collective-permute-start(f32[256]{0:T(256)S(1)} %select_add_fusion.1), channel_id=1, source_target_pairs={{1,2},{2,5},{5,6},{6,9},{9,10},{10,13},{13,14},{14,17},{17,18},{18... | collective-permute-start | bytes 3080 | tf_op jit(solution)/shard_map/ppermute | solution.py:135
  56.7 25.6 %collective-permute-start.4 = (f32[256]{0:T(256)S(1)}, f32[256]{0:T(256)S(1)}, u32[]{:S(2)}, u32[]{:S(2)}) collective-permute-start(f32[256]{0:T(256)S(1)} %select_add_fusion), channel_id=1, source_target_pairs={{1,3},{2,4},{4,5},{3,6},{5,7},{6,8},{8,9},{7,10},{9,11},{10,12},{1... | collective-permute-start | bytes 3080 | tf_op jit(solution)/shard_map/ppermute | solution.py:136
  59.5 25.3 %collective-permute-start.7 = (bf16[256,1152]{1,0:T(8,128)(2,1)S(1)}, bf16[256,1152]{1,0:T(8,128)(2,1)S(1)}, u32[]{:S(2)}, u32[]{:S(2)}) collective-permute-start(bf16[256,1152]{1,0:T(8,128)(2,1)S(1)} %fusion.7), channel_id=1, source_target_pairs={{1,0},{3,2},{4,1},{2,3},{5,4},{7,6},{8,5},{6,7},{9,8},{11,10},{12,... | collective-permute-start | bytes 1769480 | tf_op jit(solution)/shard_map/ppermute | solution.py:131

commit v4 on v3

--- a/solution.py
+++ b/solution.py
@@ -94,7 +94,7 @@
     early, image_norm = lax.optimization_barrier((image_emb, image_norm))
     near_raw = lax.ppermute(early, AXES, near_way)
     text_unit, text_norm = unit_rows(text_emb)
-    late, text_norm = lax.optimization_barrier((early, text_norm))
+    late = early
     far_raw = lax.ppermute(late, AXES, far_way)
     image_unit = image_emb.astype(jnp.float32) / image_norm
     text_unit = text_emb.astype(jnp.float32) / text_norm

time: 87.1 us -> 94.1 us (1.080)
  starting transfers between devices: 41.8 us -> 48 us
    ppermute x1, waiting for transfers between devices: 9.89 us -> 1.05 us  [shards(): far_raw = lax.ppermute(late, AXES, far_way)]
    ppermute x1, waiting for transfers between devices: 0.01 us -> 7.14 us  [shards(): text_raw = lax.ppermute(text_emb, AXES, text_way)]
    ppermute x1, starting transfers between devices: 1.99 us -> 5.17 us  [shards(): loss_near_back = lax.ppermute(loss_near, AXES, back(near_way))]
    ppermute x1, starting transfers between devices: 1.92 us -> 4.73 us  [shards(): far_back = lax.ppermute(grad_far.astype(jnp.bfloat16), AXES, back(far_way))]
    ppermute x1, starting transfers between devices: 18.5 us -> 20.8 us  [shards(): near_raw = lax.ppermute(early, AXES, near_way)]
    ppermute x1, starting transfers between devices: 4.41 us -> 2.46 us  [shards(): text_raw = lax.ppermute(text_emb, AXES, text_way)]
    ppermute x1, waiting for transfers between devices: 4.55 us -> 6.33 us  [shards(): loss_near_back = lax.ppermute(loss_near, AXES, back(near_way))]
    ppermute x1, starting transfers between devices: 1.92 us -> 3.35 us  [shards(): lax.ppermute(grad_near.astype(jnp.bfloat16), AXES, back(near_way))]
  transfers between devices with their start and end apart: 8 -> 8, of which waited for: 3 -> 4; matrix products, arithmetic and copies ran while one was open for 13% -> 11% of each run, Pallas kernels for 0% -> 0%
where the time goes in v4:
time: 94.1 us; the launch traced here: 93.7 us
  starting transfers between devices  48 us (51%)
  waiting for transfers between devices  25.7 us (27%)
  matrix products  10.8 us (11%)
  other arithmetic  7.1 us (8%)
  between operations  2.13 us (2%)
    ppermute x1, starting transfers between devices, shards(): near_raw = lax.ppermute(early, AXES, near_way)  20.8 us
    ppermute x1, waiting for transfers between devices, shards(): loss_far_back = lax.ppermute(loss_far, AXES, back(far_way))  11.1 us
    ppermute x1, starting transfers between devices, shards(): lax.ppermute(grad_other.astype(jnp.bfloat16), AXES, back(text_way))  7.31 us
    ppermute x1, waiting for transfers between devices, shards(): text_raw = lax.ppermute(text_emb, AXES, text_way)  7.14 us
    ppermute x1, waiting for transfers between devices, shards(): loss_near_back = lax.ppermute(loss_near, AXES, back(near_way))  6.33 us
    ppermute x1, starting transfers between devices, shards(): loss_near_back = lax.ppermute(loss_near, AXES, back(near_way))  5.17 us
    ppermute x1, starting transfers between devices, shards(): far_back = lax.ppermute(grad_far.astype(jnp.bfloat16), AXES, back(far_way))  4.73 us
    dot_general x6, matrix products, rows_by_rows(): lax.dot_general(a, b, (((1,), (1,)), ((), ())), preferred_element_type=jn...  4.31 us
  transfers between devices with their start and end apart: 8, of which 4 were waited for; matrix products, arithmetic and copies ran while one was open for 11% of the time, Pallas kernels for 0%

profile of v4, /device:TPU:6, one launch (start us, length us, event | category | flops | bytes accessed | tf_op | source)
XLA Modules:
  0.0 93.7 jit_solution(8248689740370177625)
XLA Ops:
  0.7 1.4 %fusion.10 = f32[256]{0:T(256)S(1)} fusion(bf16[256,1152]{1,0:T(8,128)(2,1)} %param.4), kind=kLoop, calls=%fused_computation.27 | loop fusion | flops 884480 | bytes 590848 | tf_op jit(solution)/shard_map/reduce_sum | solution.py:39
  2.0 20.8 %collective-permute-start.1 = (bf16[256,1152]{1,0:T(8,128)(2,1)}, bf16[256,1152]{1,0:T(8,128)(2,1)S(1)}, u32[]{:S(2)}, u32[]{:S(2)}) collective-permute-start(bf16[256,1152]{1,0:T(8,128)(2,1)} %param.4), channel_id=1, source_target_pairs={{2,1},{5,2},{6,5},{9,6},{10,9},{13,10},{14,13},{17,14},{18,17},{21... | collective-permute-start | bytes 1769480 | tf_op jit(solution)/shard_map/ppermute | solution.py:95
  22.9 2.2 %collective-permute-start.2 = (bf16[256,1152]{1,0:T(8,128)(2,1)}, bf16[256,1152]{1,0:T(8,128)(2,1)S(1)}, u32[]{:S(2)}, u32[]{:S(2)}) collective-permute-start(bf16[256,1152]{1,0:T(8,128)(2,1)} %param.4), channel_id=1, source_target_pairs={{3,1},{4,2},{5,4},{6,3},{7,5},{8,6},{9,8},{10,7},{11,9},{12,10},{1... | collective-permute-start | bytes 1769480 | tf_op jit(solution)/shard_map/ppermute | solution.py:98
  25.1 2.5 %collective-permute-start = (bf16[256,1152]{1,0:T(8,128)(2,1)}, bf16[256,1152]{1,0:T(8,128)(2,1)S(1)}, u32[]{:S(2)}, u32[]{:S(2)}) collective-permute-start(bf16[256,1152]{1,0:T(8,128)(2,1)} %param.5), channel_id=1, source_target_pairs={{0,1},{2,3},{1,4},{3,2},{4,5},{6,7},{5,8},{7,6},{8,9},{10,11},{9,1... | collective-permute-start | bytes 1769480 | tf_op jit(solution)/shard_map/ppermute | solution.py:92
  27.5 1.3 %fusion.11 = f32[256]{0:T(256)S(1)} fusion(bf16[256,1152]{1,0:T(8,128)(2,1)} %param.5), kind=kLoop, calls=%fused_computation.28 | loop fusion | flops 884480 | bytes 590848 | tf_op jit(solution)/shard_map/reduce_sum | solution.py:39
  30.4 1.3 %fusion.25 = (f32[256]{0:T(256)S(1)}, f32[256,256]{0,1:T(8,128)}) fusion(f32[]{:T(128)} %bitcast.21, bf16[256,1152]{1,0:T(8,128)(2,1)S(1)} %fusion.50, f32[256]{0:T(256)S(1)} %add_sqrt_fusion.4, bf16[256,1152]{1,0:T(8,128)(2,1)S(1)} %copy-done.1, f32[]{:T(128)} %bitcast.10), kind=kOutput, calls=%fused_computation.59 | convolution fusion | flops 152731392 | bytes 1443848 | tf_op jit(solution)/shard_map/dot_general | solution.py:52
  31.7 1.5 %fusion.52 = f32[256,1152]{1,0:T(8,128)S(1)} fusion(f32[256,256]{0,1:T(8,128)} %get-tuple-element.22, f32[256]{0:T(256)S(1)} %add_sqrt_fusion.4, bf16[256,1152]{1,0:T(8,128)(2,1)S(1)} %copy-done.1), kind=kOutput, calls=%fused_computation.92 | convolution fusion | flops 152403968 | bytes 2032640 | tf_op jit(solution)/shard_map/dot_general | solution.py:56
  33.6 7.1 %collective-permute-done = bf16[256,1152]{1,0:T(8,128)(2,1)S(1)} collective-permute-done((bf16[256,1152]{1,0:T(8,128)(2,1)}, bf16[256,1152]{1,0:T(8,128)(2,1)S(1)}, u32[]{:S(2)}, u32[]{:S(2)}) %collective-permute-start) | collective-permute-done | bytes 589856 | tf_op jit(solution)/shard_map/ppermute | solution.py:92
  41.1 0.6 fusion.26
  42.2 1.0 %collective-permute-done.2 = bf16[256,1152]{1,0:T(8,128)(2,1)S(1)} collective-permute-done((bf16[256,1152]{1,0:T(8,128)(2,1)}, bf16[256,1152]{1,0:T(8,128)(2,1)S(1)}, u32[]{:S(2)}, u32[]{:S(2)}) %collective-permute-start.2) | collective-permute-done | bytes 589856 | tf_op jit(solution)/shard_map/ppermute | solution.py:98
  43.4 0.6 fusion.27
  44.4 0.6 fusion.28
  45.1 0.6 fusion.29
  46.1 0.6 fusion.30
  48.0 4.7 %collective-permute-start.6 = (bf16[256,1152]{1,0:T(8,128)(2,1)S(1)}, bf16[256,1152]{1,0:T(8,128)(2,1)S(1)}, u32[]{:S(2)}, u32[]{:S(2)}) collective-permute-start(bf16[256,1152]{1,0:T(8,128)(2,1)S(1)} %fusion.8), channel_id=1, source_target_pairs={{1,3},{2,4},{4,5},{3,6},{5,7},{6,8},{8,9},{7,10},{9,11},{10,12},{1... | collective-permute-start | bytes 1769480 | tf_op jit(solution)/shard_map/ppermute | solution.py:127
  53.2 3.3 %collective-permute-start.5 = (bf16[256,1152]{1,0:T(8,128)(2,1)S(1)}, bf16[256,1152]{1,0:T(8,128)(2,1)S(1)}, u32[]{:S(2)}, u32[]{:S(2)}) collective-permute-start(bf16[256,1152]{1,0:T(8,128)(2,1)S(1)} %fusion.9), channel_id=1, source_target_pairs={{1,2},{2,5},{5,6},{6,9},{9,10},{10,13},{13,14},{14,17},{17,18},{18... | collective-permute-start | bytes 1769480 | tf_op jit(solution)/shard_map/ppermute | solution.py:118
  56.6 5.2 %collective-permute-start.3 = (f32[256]{0:T(256)S(1)}, f32[256]{0:T(256)S(1)}, u32[]{:S(2)}, u32[]{:S(2)}) collective-permute-start(f32[256]{0:T(256)S(1)} %select_add_fusion.1), channel_id=1, source_target_pairs={{1,2},{2,5},{5,6},{6,9},{9,10},{10,13},{13,14},{14,17},{17,18},{18... | collective-permute-start | bytes 3080 | tf_op jit(solution)/shard_map/ppermute | solution.py:135
  61.7 1.9 %collective-permute-start.4 = (f32[256]{0:T(256)S(1)}, f32[256]{0:T(256)S(1)}, u32[]{:S(2)}, u32[]{:S(2)}) collective-permute-start(f32[256]{0:T(256)S(1)} %select_add_fusion), channel_id=1, source_target_pairs={{1,3},{2,4},{4,5},{3,6},{5,7},{6,8},{8,9},{7,10},{9,11},{10,12},{1... | collective-permute-start | bytes 3080 | tf_op jit(solution)/shard_map/ppermute | solution.py:136
  64.6 7.3 %collective-permute-start.7 = (bf16[256,1152]{1,0:T(8,128)(2,1)S(1)}, bf16[256,1152]{1,0:T(8,128)(2,1)S(1)}, u32[]{:S(2)}, u32[]{:S(2)}) collective-permute-start(bf16[256,1152]{1,0:T(8,128)(2,1)S(1)} %fusion.7), channel_id=1, source_target_pairs={{1,0},{3,2},{4,1},{2,3},{5,4},{7,6},{8,5},{6,7},{9,8},{11,10},{12,... | collective-permute-start | bytes 1769480 | tf_op jit(solution)/shard_map/ppermute | solution.py:131
  71.9 6.3 %collective-permute-done.3 = f32[256]{0:T(256)S(1)} collective-permute-done((f32[256]{0:T(256)S(1)}, f32[256]{0:T(256)S(1)}, u32[]{:S(2)}, u32[]{:S(2)}) %collective-permute-start.3) | collective-permute-done | bytes 1056 | tf_op jit(solution)/shard_map/ppermute | solution.py:135
  78.2 11.1 %collective-permute-done.4 = f32[256]{0:T(256)S(1)} collective-permute-done((f32[256]{0:T(256)S(1)}, f32[256]{0:T(256)S(1)}, u32[]{:S(2)}, u32[]{:S(2)}) %collective-permute-start.4) | collective-permute-done | bytes 1056 | tf_op jit(solution)/shard_map/ppermute | solution.py:136
  89.9 0.7 multiply_reduce_fusion.1
  90.7 1.3 %subtract_divide_fusion.1 = f32[256,1152]{1,0:T(8,128)} fusion(f32[256,1152]{1,0:T(8,128)S(1)} %get-tuple-element.26, f32[256]{0:T(256)S(1)} %get-tuple-element.25, f32[256]{0:T(256)S(1)} %add_sqrt_fusion.4, bf16[256,1152]{1,0:T(8,128)(2,1)S(1)} %copy-done.1), kind=kLoop, calls=%fused_computation.38 | loop fusion | flops 1474560 | bytes 2951168 | tf_op jit(solution)/shard_map/div | solution.py:48
  92.3 1.4 %subtract_divide_fusion = f32[256,1152]{1,0:T(8,128)} fusion(f32[256,1152]{1,0:T(8,128)S(1)} %fusion, bf16[256,1152]{1,0:T(8,128)(2,1)S(1)} %collective-permute-done.7, f32[256]{0:T(256)S(1)} %multiply_reduce_fusion, f32[256]{0:T(256)S(1)} %add_sqrt_fusion.3, bf16[256,1152]{1,0:T(8,128)(2,1)S(1)} %copy-done), kind=kLoop, calls=%fused_computation.35 | loop fusion | flops 2064384 | bytes 3540992 | tf_op jit(solution)/shard_map/div | solution.py:48
  (33 shorter events, 6.1 us)
Async XLA Ops:
  0.6 29.7 %copy-start.1 = (bf16[256,1152]{1,0:T(8,128)(2,1)S(1)}, bf16[256,1152]{1,0:T(8,128)(2,1)}, u32[]{:S(2)}) copy-start(bf16[256,1152]{1,0:T(8,128)(2,1)} %param.4) | copy-start | bytes 1769476
  0.6 29.5 %copy-start = (bf16[256,1152]{1,0:T(8,128)(2,1)S(1)}, bf16[256,1152]{1,0:T(8,128)(2,1)}, u32[]{:S(2)}) copy-start(bf16[256,1152]{1,0:T(8,128)(2,1)} %param.5) | copy-start | bytes 1769476
  2.0 38.9 %collective-permute-start.1 = (bf16[256,1152]{1,0:T(8,128)(2,1)}, bf16[256,1152]{1,0:T(8,128)(2,1)S(1)}, u32[]{:S(2)}, u32[]{:S(2)}) collective-permute-start(bf16[256,1152]{1,0:T(8,128)(2,1)} %param.4), channel_id=1, source_target_pairs={{2,1},{5,2},{6,5},{9,6},{10,9},{13,10},{14,13},{17,14},{18,17},{21... | collective-permute-start | bytes 1769480 | tf_op jit(solution)/shard_map/ppermute | solution.py:95
  22.9 20.4 %collective-permute-start.2 = (bf16[256,1152]{1,0:T(8,128)(2,1)}, bf16[256,1152]{1,0:T(8,128)(2,1)S(1)}, u32[]{:S(2)}, u32[]{:S(2)}) collective-permute-start(bf16[256,1152]{1,0:T(8,128)(2,1)} %param.4), channel_id=1, source_target_pairs={{3,1},{4,2},{5,4},{6,3},{7,5},{8,6},{9,8},{10,7},{11,9},{12,10},{1... | collective-permute-start | bytes 1769480 | tf_op jit(solution)/shard_map/ppermute | solution.py:98
  25.1 15.6 %collective-permute-start = (bf16[256,1152]{1,0:T(8,128)(2,1)}, bf16[256,1152]{1,0:T(8,128)(2,1)S(1)}, u32[]{:S(2)}, u32[]{:S(2)}) collective-permute-start(bf16[256,1152]{1,0:T(8,128)(2,1)} %param.5), channel_id=1, source_target_pairs={{0,1},{2,3},{1,4},{3,2},{4,5},{6,7},{5,8},{7,6},{8,9},{10,11},{9,1... | collective-permute-start | bytes 1769480 | tf_op jit(solution)/shard_map/ppermute | solution.py:92
  31.7 1.5 %copy-start.2 = (f32[256,256]{0,1:T(8,128)S(1)}, f32[256,256]{0,1:T(8,128)}, u32[]{:S(2)}) copy-start(f32[256,256]{0,1:T(8,128)} %get-tuple-element.22) | copy-start | bytes 786436
  48.0 41.9 %collective-permute-start.6 = (bf16[256,1152]{1,0:T(8,128)(2,1)S(1)}, bf16[256,1152]{1,0:T(8,128)(2,1)S(1)}, u32[]{:S(2)}, u32[]{:S(2)}) collective-permute-start(bf16[256,1152]{1,0:T(8,128)(2,1)S(1)} %fusion.8), channel_id=1, source_target_pairs={{1,3},{2,4},{4,5},{3,6},{5,7},{6,8},{8,9},{7,10},{9,11},{10,12},{1... | collective-permute-start | bytes 1769480 | tf_op jit(solution)/shard_map/ppermute | solution.py:127
  53.2 36.7 %collective-permute-start.5 = (bf16[256,1152]{1,0:T(8,128)(2,1)S(1)}, bf16[256,1152]{1,0:T(8,128)(2,1)S(1)}, u32[]{:S(2)}, u32[]{:S(2)}) collective-permute-start(bf16[256,1152]{1,0:T(8,128)(2,1)S(1)} %fusion.9), channel_id=1, source_target_pairs={{1,2},{2,5},{5,6},{6,9},{9,10},{10,13},{13,14},{14,17},{17,18},{18... | collective-permute-start | bytes 1769480 | tf_op jit(solution)/shard_map/ppermute | solution.py:118
  56.6 21.6 %collective-permute-start.3 = (f32[256]{0:T(256)S(1)}, f32[256]{0:T(256)S(1)}, u32[]{:S(2)}, u32[]{:S(2)}) collective-permute-start(f32[256]{0:T(256)S(1)} %select_add_fusion.1), channel_id=1, source_target_pairs={{1,2},{2,5},{5,6},{6,9},{9,10},{10,13},{13,14},{14,17},{17,18},{18... | collective-permute-start | bytes 3080 | tf_op jit(solution)/shard_map/ppermute | solution.py:135
  61.7 27.6 %collective-permute-start.4 = (f32[256]{0:T(256)S(1)}, f32[256]{0:T(256)S(1)}, u32[]{:S(2)}, u32[]{:S(2)}) collective-permute-start(f32[256]{0:T(256)S(1)} %select_add_fusion), channel_id=1, source_target_pairs={{1,3},{2,4},{4,5},{3,6},{5,7},{6,8},{8,9},{7,10},{9,11},{10,12},{1... | collective-permute-start | bytes 3080 | tf_op jit(solution)/shard_map/ppermute | solution.py:136
  64.6 27.4 %collective-permute-start.7 = (bf16[256,1152]{1,0:T(8,128)(2,1)S(1)}, bf16[256,1152]{1,0:T(8,128)(2,1)S(1)}, u32[]{:S(2)}, u32[]{:S(2)}) collective-permute-start(bf16[256,1152]{1,0:T(8,128)(2,1)S(1)} %fusion.7), channel_id=1, source_target_pairs={{1,0},{3,2},{4,1},{2,3},{5,4},{7,6},{8,5},{6,7},{9,8},{11,10},{12,... | collective-permute-start | bytes 1769480 | tf_op jit(solution)/shard_map/ppermute | solution.py:131

commit v5 on v3

--- a/solution.py
+++ b/solution.py
@@ -115,7 +115,6 @@
         jnp.dot(c_on, texts, preferred_element_type=jnp.float32)
         + jnp.dot(c_rn, other, preferred_element_type=jnp.float32)
     )
-    near_back = lax.ppermute(grad_near.astype(jnp.bfloat16), AXES, back(near_way))
 
     far = unit_bf(far_raw)
     c_of, l_of = off_terms(far, texts, s_val, b_val, hub | (leaf & ~seam))
@@ -124,11 +123,15 @@
         jnp.dot(c_of, texts, preferred_element_type=jnp.float32)
         + jnp.dot(c_rf, other, preferred_element_type=jnp.float32)
     )
-    far_back = lax.ppermute(grad_far.astype(jnp.bfloat16), AXES, back(far_way))
     grad_other = s_val * (
         columns_by_rows(c_ri, images) + columns_by_rows(c_rn, near) + columns_by_rows(c_rf, far)
     )
-    text_back = lax.ppermute(grad_other.astype(jnp.bfloat16), AXES, back(text_way))
+    near_sent, far_sent, other_sent = lax.optimization_barrier(
+        (grad_near.astype(jnp.bfloat16), grad_far.astype(jnp.bfloat16), grad_other.astype(jnp.bfloat16))
+    )
+    text_back = lax.ppermute(other_sent, AXES, back(text_way))
+    far_back = lax.ppermute(far_sent, AXES, back(far_way))
+    near_back = lax.ppermute(near_sent, AXES, back(near_way))
 
     grad_y = s_val * (grad_y + columns_by_rows(c_on, near) + columns_by_rows(c_of, far))
     grad_y, loss_near, loss_far = lax.optimization_barrier((grad_y, l_on + l_rn, l_of + l_rf))

time: 87.1 us -> 89.3 us (1.025); the launches traced: 86.6 us -> 87.9 us
  waiting for transfers between devices: 24.9 us -> 27.8 us
  matrix products: 10.8 us -> 9.12 us
    ppermute x1, waiting for transfers between devices: 10.4 us -> 0.01 us  [shards(): loss_far_back = lax.ppermute(loss_far, AXES, back(far_way))]
    ppermute x1, waiting for transfers between devices: 4.55 us -> 11.2 us  [shards(): loss_near_back = lax.ppermute(loss_near, AXES, back(near_way))]
    ppermute x3, waiting for transfers between devices: 0.01 us -> 4.57 us  [the longest x1 4.56 us: shards(): text_back = lax.ppermute(other_sent, AXES, back(text_way))]
    ppermute x1, waiting for transfers between devices: 9.89 us -> 11.4 us  [shards(): far_raw = lax.ppermute(late, AXES, far_way)]
    dot_general x6, matrix products: 3.67 us -> 2.66 us  [columns_by_rows(): lax.dot_general(a, b, (((0,), (0,)), ((), ())), preferred_element_type=jn...]
  transfers between devices with their start and end apart: 8 -> 8, of which waited for: 3 -> 4; matrix products, arithmetic and copies ran while one was open for 13% -> 10% of each run, Pallas kernels for 0% -> 0%
where the time goes in v5:
time: 89.3 us; the launch traced here: 87.9 us
  starting transfers between devices  41.8 us (47%)
  waiting for transfers between devices  27.8 us (31%)
  matrix products  9.12 us (10%)
  other arithmetic  6.99 us (8%)
  between operations  2.17 us (2%)
    ppermute x1, starting transfers between devices, shards(): near_raw = lax.ppermute(early, AXES, near_way)  18.5 us
    ppermute x1, waiting for transfers between devices, shards(): far_raw = lax.ppermute(late, AXES, far_way)  11.4 us
    ppermute x1, waiting for transfers between devices, shards(): loss_near_back = lax.ppermute(loss_near, AXES, back(near_way))  11.2 us
    ppermute x1, starting transfers between devices, shards(): text_back = lax.ppermute(other_sent, AXES, back(text_way))  7.77 us
    ppermute x1, waiting for transfers between devices, shards(): text_back = lax.ppermute(other_sent, AXES, back(text_way))  4.56 us
    ppermute x1, starting transfers between devices, shards(): text_raw = lax.ppermute(text_emb, AXES, text_way)  4.41 us
    dot_general x6, matrix products, rows_by_rows(): lax.dot_general(a, b, (((1,), (1,)), ((), ())), preferred_element_type=jn...  3.64 us
    ppermute x1, starting transfers between devices, shards(): far_raw = lax.ppermute(late, AXES, far_way)  3.38 us
  transfers between devices with their start and end apart: 8, of which 4 were waited for; matrix products, arithmetic and copies ran while one was open for 10% of the time, Pallas kernels for 0%

profile of v5, /device:TPU:6, one launch (start us, length us, event | category | flops | bytes accessed | tf_op | source)
XLA Modules:
  0.0 87.9 jit_solution(3184597197475549408)
XLA Ops:
  0.7 4.4 %collective-permute-start = (bf16[256,1152]{1,0:T(8,128)(2,1)}, bf16[256,1152]{1,0:T(8,128)(2,1)S(1)}, u32[]{:S(2)}, u32[]{:S(2)}) collective-permute-start(bf16[256,1152]{1,0:T(8,128)(2,1)} %param.5), channel_id=1, source_target_pairs={{0,1},{2,3},{1,4},{3,2},{4,5},{6,7},{5,8},{7,6},{8,9},{10,11},{9,1... | collective-permute-start | bytes 1769480 | tf_op jit(solution)/shard_map/ppermute | solution.py:92
  5.1 1.3 %fusion.10 = f32[256]{0:T(256)S(1)} fusion(bf16[256,1152]{1,0:T(8,128)(2,1)} %param.4), kind=kLoop, calls=%fused_computation.27 | loop fusion | flops 884480 | bytes 590848 | tf_op jit(solution)/shard_map/reduce_sum | solution.py:39
  6.3 18.5 %collective-permute-start.1 = (bf16[256,1152]{1,0:T(8,128)(2,1)}, bf16[256,1152]{1,0:T(8,128)(2,1)S(1)}, u32[]{:S(2)}, u32[]{:S(2)}) collective-permute-start(bf16[256,1152]{1,0:T(8,128)(2,1)} %param.4), channel_id=1, source_target_pairs={{2,1},{5,2},{6,5},{9,6},{10,9},{13,10},{14,13},{17,14},{18,17},{21... | collective-permute-start | bytes 1769480 | tf_op jit(solution)/shard_map/ppermute | solution.py:95
  24.8 1.3 %fusion.11 = f32[256]{0:T(256)S(1)} fusion(bf16[256,1152]{1,0:T(8,128)(2,1)} %param.5), kind=kLoop, calls=%fused_computation.28 | loop fusion | flops 884480 | bytes 590848 | tf_op jit(solution)/shard_map/reduce_sum | solution.py:39
  26.1 3.4 %collective-permute-start.2 = (bf16[256,1152]{1,0:T(8,128)(2,1)S(1)}, bf16[256,1152]{1,0:T(8,128)(2,1)S(1)}, u32[]{:S(2)}, u32[]{:S(2)}) collective-permute-start(bf16[256,1152]{1,0:T(8,128)(2,1)S(1)} %copy-done.1), channel_id=1, source_target_pairs={{3,1},{4,2},{5,4},{6,3},{7,5},{8,6},{9,8},{10,7},{11,9},{12,10},{1... | collective-permute-start | bytes 1769480 | tf_op jit(solution)/shard_map/ppermute | solution.py:98
  31.1 0.6 fusion.25
  32.4 0.6 collective-permute-done.1
  33.2 0.6 fusion.26
  34.3 11.4 %collective-permute-done.2 = bf16[256,1152]{1,0:T(8,128)(2,1)S(1)} collective-permute-done((bf16[256,1152]{1,0:T(8,128)(2,1)S(1)}, bf16[256,1152]{1,0:T(8,128)(2,1)S(1)}, u32[]{:S(2)}, u32[]{:S(2)}) %collective-permute-start.2) | collective-permute-done | bytes 589856 | tf_op jit(solution)/shard_map/ppermute | solution.py:98
  45.8 0.6 fusion.29
  46.8 0.6 fusion.27
  47.8 0.6 fusion.28
  48.9 0.6 fusion.30
  50.8 1.9 %collective-permute-start.5 = (bf16[256,1152]{1,0:T(8,128)(2,1)S(1)}, bf16[256,1152]{1,0:T(8,128)(2,1)S(1)}, u32[]{:S(2)}, u32[]{:S(2)}) collective-permute-start(bf16[256,1152]{1,0:T(8,128)(2,1)S(1)} %fusion.9), channel_id=1, source_target_pairs={{1,2},{2,5},{5,6},{6,9},{9,10},{10,13},{13,14},{14,17},{17,18},{18... | collective-permute-start | bytes 1769480 | tf_op jit(solution)/shard_map/ppermute | solution.py:134
  52.8 1.9 %collective-permute-start.6 = (bf16[256,1152]{1,0:T(8,128)(2,1)S(1)}, bf16[256,1152]{1,0:T(8,128)(2,1)S(1)}, u32[]{:S(2)}, u32[]{:S(2)}) collective-permute-start(bf16[256,1152]{1,0:T(8,128)(2,1)S(1)} %fusion.8), channel_id=1, source_target_pairs={{1,3},{2,4},{4,5},{3,6},{5,7},{6,8},{8,9},{7,10},{9,11},{10,12},{1... | collective-permute-start | bytes 1769480 | tf_op jit(solution)/shard_map/ppermute | solution.py:133
  55.6 2.0 %collective-permute-start.3 = (f32[256]{0:T(256)S(1)}, f32[256]{0:T(256)S(1)}, u32[]{:S(2)}, u32[]{:S(2)}) collective-permute-start(f32[256]{0:T(256)S(1)} %select_add_fusion.1), channel_id=1, source_target_pairs={{1,2},{2,5},{5,6},{6,9},{9,10},{10,13},{13,14},{14,17},{17,18},{18... | collective-permute-start | bytes 3080 | tf_op jit(solution)/shard_map/ppermute | solution.py:138
  57.6 1.9 %collective-permute-start.4 = (f32[256]{0:T(256)S(1)}, f32[256]{0:T(256)S(1)}, u32[]{:S(2)}, u32[]{:S(2)}) collective-permute-start(f32[256]{0:T(256)S(1)} %select_add_fusion), channel_id=1, source_target_pairs={{1,3},{2,4},{4,5},{3,6},{5,7},{6,8},{8,9},{7,10},{9,11},{10,12},{1... | collective-permute-start | bytes 3080 | tf_op jit(solution)/shard_map/ppermute | solution.py:139
  60.0 7.8 %collective-permute-start.7 = (bf16[256,1152]{1,0:T(8,128)(2,1)S(1)}, bf16[256,1152]{1,0:T(8,128)(2,1)S(1)}, u32[]{:S(2)}, u32[]{:S(2)}) collective-permute-start(bf16[256,1152]{1,0:T(8,128)(2,1)S(1)} %fusion.7), channel_id=1, source_target_pairs={{1,0},{3,2},{4,1},{2,3},{5,4},{7,6},{8,5},{6,7},{9,8},{11,10},{12,... | collective-permute-start | bytes 1769480 | tf_op jit(solution)/shard_map/ppermute | solution.py:132
  67.7 11.2 %collective-permute-done.3 = f32[256]{0:T(256)S(1)} collective-permute-done((f32[256]{0:T(256)S(1)}, f32[256]{0:T(256)S(1)}, u32[]{:S(2)}, u32[]{:S(2)}) %collective-permute-start.3) | collective-permute-done | bytes 1056 | tf_op jit(solution)/shard_map/ppermute | solution.py:138
  79.0 0.6 add_multiply_fusion
  79.5 0.7 multiply_reduce_fusion.1
  80.3 1.3 %subtract_divide_fusion.1 = f32[256,1152]{1,0:T(8,128)} fusion(f32[256,1152]{1,0:T(8,128)S(1)} %get-tuple-element.36, f32[256]{0:T(256)S(1)} %get-tuple-element.35, f32[256]{0:T(256)S(1)} %add_sqrt_fusion.4, bf16[256,1152]{1,0:T(8,128)(2,1)S(1)} %copy-done.1), kind=kLoop, calls=%fused_computation.38 | loop fusion | flops 1474560 | bytes 2951168 | tf_op jit(solution)/shard_map/div | solution.py:48
  81.6 4.6 %collective-permute-done.7 = bf16[256,1152]{1,0:T(8,128)(2,1)S(1)} collective-permute-done((bf16[256,1152]{1,0:T(8,128)(2,1)S(1)}, bf16[256,1152]{1,0:T(8,128)(2,1)S(1)}, u32[]{:S(2)}, u32[]{:S(2)}) %collective-permute-start.7) | collective-permute-done | bytes 589856 | tf_op jit(solution)/shard_map/ppermute | solution.py:132
  86.5 1.4 %subtract_divide_fusion = f32[256,1152]{1,0:T(8,128)} fusion(f32[256,1152]{1,0:T(8,128)S(1)} %fusion, bf16[256,1152]{1,0:T(8,128)(2,1)S(1)} %collective-permute-done.7, f32[256]{0:T(256)S(1)} %multiply_reduce_fusion, f32[256]{0:T(256)S(1)} %add_sqrt_fusion.3, bf16[256,1152]{1,0:T(8,128)(2,1)S(1)} %copy-done), kind=kLoop, calls=%fused_computation.35 | loop fusion | flops 2064384 | bytes 3540992 | tf_op jit(solution)/shard_map/div | solution.py:48
  (31 shorter events, 6.0 us)
Async XLA Ops:
  0.6 28.9 %copy-start = (bf16[256,1152]{1,0:T(8,128)(2,1)S(1)}, bf16[256,1152]{1,0:T(8,128)(2,1)}, u32[]{:S(2)}) copy-start(bf16[256,1152]{1,0:T(8,128)(2,1)} %param.5) | copy-start | bytes 1769476
  0.6 25.5 %copy-start.1 = (bf16[256,1152]{1,0:T(8,128)(2,1)S(1)}, bf16[256,1152]{1,0:T(8,128)(2,1)}, u32[]{:S(2)}) copy-start(bf16[256,1152]{1,0:T(8,128)(2,1)} %param.4) | copy-start | bytes 1769476
  0.7 31.5 %collective-permute-start = (bf16[256,1152]{1,0:T(8,128)(2,1)}, bf16[256,1152]{1,0:T(8,128)(2,1)S(1)}, u32[]{:S(2)}, u32[]{:S(2)}) collective-permute-start(bf16[256,1152]{1,0:T(8,128)(2,1)} %param.5), channel_id=1, source_target_pairs={{0,1},{2,3},{1,4},{3,2},{4,5},{6,7},{5,8},{7,6},{8,9},{10,11},{9,1... | collective-permute-start | bytes 1769480 | tf_op jit(solution)/shard_map/ppermute | solution.py:92
  6.3 26.7 %collective-permute-start.1 = (bf16[256,1152]{1,0:T(8,128)(2,1)}, bf16[256,1152]{1,0:T(8,128)(2,1)S(1)}, u32[]{:S(2)}, u32[]{:S(2)}) collective-permute-start(bf16[256,1152]{1,0:T(8,128)(2,1)} %param.4), channel_id=1, source_target_pairs={{2,1},{5,2},{6,5},{9,6},{10,9},{13,10},{14,13},{17,14},{18,17},{21... | collective-permute-start | bytes 1769480 | tf_op jit(solution)/shard_map/ppermute | solution.py:95
  26.1 19.5 %collective-permute-start.2 = (bf16[256,1152]{1,0:T(8,128)(2,1)S(1)}, bf16[256,1152]{1,0:T(8,128)(2,1)S(1)}, u32[]{:S(2)}, u32[]{:S(2)}) collective-permute-start(bf16[256,1152]{1,0:T(8,128)(2,1)S(1)} %copy-done.1), channel_id=1, source_target_pairs={{3,1},{4,2},{5,4},{6,3},{7,5},{8,6},{9,8},{10,7},{11,9},{12,10},{1... | collective-permute-start | bytes 1769480 | tf_op jit(solution)/shard_map/ppermute | solution.py:98
  50.8 28.7 %collective-permute-start.5 = (bf16[256,1152]{1,0:T(8,128)(2,1)S(1)}, bf16[256,1152]{1,0:T(8,128)(2,1)S(1)}, u32[]{:S(2)}, u32[]{:S(2)}) collective-permute-start(bf16[256,1152]{1,0:T(8,128)(2,1)S(1)} %fusion.9), channel_id=1, source_target_pairs={{1,2},{2,5},{5,6},{6,9},{9,10},{10,13},{13,14},{14,17},{17,18},{18... | collective-permute-start | bytes 1769480 | tf_op jit(solution)/shard_map/ppermute | solution.py:134
  52.8 26.8 %collective-permute-start.6 = (bf16[256,1152]{1,0:T(8,128)(2,1)S(1)}, bf16[256,1152]{1,0:T(8,128)(2,1)S(1)}, u32[]{:S(2)}, u32[]{:S(2)}) collective-permute-start(bf16[256,1152]{1,0:T(8,128)(2,1)S(1)} %fusion.8), channel_id=1, source_target_pairs={{1,3},{2,4},{4,5},{3,6},{5,7},{6,8},{8,9},{7,10},{9,11},{10,12},{1... | collective-permute-start | bytes 1769480 | tf_op jit(solution)/shard_map/ppermute | solution.py:133
  55.6 23.3 %collective-permute-start.3 = (f32[256]{0:T(256)S(1)}, f32[256]{0:T(256)S(1)}, u32[]{:S(2)}, u32[]{:S(2)}) collective-permute-start(f32[256]{0:T(256)S(1)} %select_add_fusion.1), channel_id=1, source_target_pairs={{1,2},{2,5},{5,6},{6,9},{9,10},{10,13},{13,14},{14,17},{17,18},{18... | collective-permute-start | bytes 3080 | tf_op jit(solution)/shard_map/ppermute | solution.py:138
  57.6 21.3 %collective-permute-start.4 = (f32[256]{0:T(256)S(1)}, f32[256]{0:T(256)S(1)}, u32[]{:S(2)}, u32[]{:S(2)}) collective-permute-start(f32[256]{0:T(256)S(1)} %select_add_fusion), channel_id=1, source_target_pairs={{1,3},{2,4},{4,5},{3,6},{5,7},{6,8},{8,9},{7,10},{9,11},{10,12},{1... | collective-permute-start | bytes 3080 | tf_op jit(solution)/shard_map/ppermute | solution.py:139
  60.0 26.2 %collective-permute-start.7 = (bf16[256,1152]{1,0:T(8,128)(2,1)S(1)}, bf16[256,1152]{1,0:T(8,128)(2,1)S(1)}, u32[]{:S(2)}, u32[]{:S(2)}) collective-permute-start(bf16[256,1152]{1,0:T(8,128)(2,1)S(1)} %fusion.7), channel_id=1, source_target_pairs={{1,0},{3,2},{4,1},{2,3},{5,4},{7,6},{8,5},{6,7},{9,8},{11,10},{12,... | collective-permute-start | bytes 1769480 | tf_op jit(solution)/shard_map/ppermute | solution.py:132
